TPU v7x, 256 devices: a whole 4x4x8 slice. The times are simulated.
256 devices in a mesh: gx: 16 (over x, y), gy: 8 (over z), ta: 2 (over core).
Axes of the slice: x: 4, y: 4, z: 8, core: 2. Of those that a mesh axis runs over, the one named last changes fastest.
Arguments:
- movie: bfloat16 [16, 8, 128, 32, 1024], P('gx', 'gy', None, 'ta'), may hold values from -4 to 6
- pieces: bfloat16 [16, 8, 128, 16, 1024], P('gx', 'gy'), may hold values from 0 to 0.053955078
- owner: int32 [16, 8, 2048, 1], P('gx', 'gy'), may hold values from 0 to 127; in each aligned block of 2048 rows (0 to 2047, 2048 to 4095, ..., all dimensions but the last counted through in order) at most 64 rows name the same one
- block_offset: int32 [16, 8, 2048], P('gx', 'gy'), may hold values from 0 to 1023
- light: bfloat16 [16, 8, 128, 1024], P('gx', 'gy'), may hold values from 0.3 to 6.5, as said below
- traces: float32 [32, 131072], P('ta', ('gx', 'gy')), may hold values from 0 to 2
- ar_first: float32 [131072], P(('gx', 'gy')), may hold values from 0.8 to 1.4
- ar_second: float32 [131072], P(('gx', 'gy')), may hold values from -0.45 to -0.05
- mixing: bfloat16 [32, 32, 131072], P(None, None, ('gx', 'gy')), may hold values from -0.13 to 0.43
Outputs:
- traces_out: float32 [32, 131072], P('ta', ('gx', 'gy'))
- background: float32 [32], P('ta')
Inputs may be any that keep to these rules, and one draw needn't show every extreme that they name: At most 64 slots of one tile name the same owner, and some tile has exactly 64 slots for one owner. `light`: Positive.
All inputs are finite; a program needn't handle non-finite values.
Results may differ from a plain program's by a relative error of at most 0.011.
Values may be sent and summed in bfloat16 or wider, within the bound.
A program may use at most 64 MiB of HBM per device.

v0:
```python
import jax
import jax.numpy as jnp
from jax import lax
from jax.sharding import PartitionSpec as P

DECONV_ITERS = 3
PASSES = 2


def forward_filter(values, first_lag, second_lag):
    prev_one = jnp.concatenate([jnp.zeros_like(values[:1]), values[:-1]], 0)
    prev_two = jnp.concatenate([jnp.zeros_like(values[:2]), values[:-2]], 0)
    return values - first_lag * prev_one - second_lag * prev_two


def adjoint_filter(values, first_lag, second_lag):
    next_one = jnp.concatenate([values[1:], jnp.zeros_like(values[:1])], 0)
    next_two = jnp.concatenate([values[2:], jnp.zeros_like(values[:2])], 0)
    return values - first_lag * next_one - second_lag * next_two


def deconvolve(target, first_lag, second_lag, inverse_block):
    inverse_wide = inverse_block.astype(jnp.float32)
    latest = target
    scaled_dual = jnp.zeros_like(target)
    for sweep in range(DECONV_ITERS):
        filtered = forward_filter(latest, first_lag, second_lag)
        spikes = jnp.maximum(filtered + scaled_dual, 0.0)
        scaled_dual = scaled_dual + filtered - spikes
        driven = target + adjoint_filter(spikes - scaled_dual, first_lag, second_lag)
        latest = jnp.sum(inverse_wide * driven[None, :, :], axis=1)
    return latest


def deliver_copies(outgoing):
    return lax.all_to_all(outgoing, ("gx", "gy"), split_axis=1, concat_axis=1, tiled=True)


def deliver_terms(outbox, norm_row):
    return (
        lax.all_to_all(outbox, ("gx", "gy"), split_axis=1, concat_axis=1, tiled=True),
        lax.all_to_all(norm_row, ("gx", "gy"), split_axis=1, concat_axis=1, tiled=True),
    )


def refine(estimate, ar_first, ar_second, mixing):
    frame_rows = estimate.shape[0]
    all_frames = lax.all_gather(estimate, "ta", axis=0, tiled=True)
    cleaned = deconvolve(all_frames, ar_first, ar_second, mixing)
    return lax.dynamic_slice_in_dim(cleaned, lax.axis_index("ta") * frame_rows, frame_rows, 0)


def body(movie, pieces, owner, block_offset, light, traces, ar_first, ar_second, mixing):
    along_x = lax.axis_size("gx")
    owners = along_x * lax.axis_size("gy")
    frame_rows = movie.shape[3]
    cell_count = movie.shape[2]
    per_cell = pieces.shape[3]
    slot_count = cell_count * per_cell
    own_count = traces.shape[1]
    capacity = max(2, 4 * slot_count // owners)
    target = owner[0, 0, :, 0]
    wanted = block_offset[0, 0]
    matches = (target[:, None] == jnp.arange(owners, dtype=jnp.int32)[None, :]).astype(jnp.int32)
    placed = jnp.sum(jnp.cumsum(matches, 0) * matches, 1) - 1
    column = target * capacity + placed
    request = jnp.full((1, owners * capacity), -1, jnp.int32).at[0, column].set(wanted)
    asked_rows = lax.all_to_all(request, ("gx", "gy"), split_axis=1, concat_axis=1, tiled=True)[0]
    lookup = jnp.where(asked_rows >= 0, asked_rows, own_count)
    tile_pieces = pieces[0, 0]
    tile_movie = movie[0, 0]
    light_wide = light[0, 0].astype(jnp.float32)
    piece_norm = jnp.sum(jnp.square(tile_pieces.astype(jnp.float32)), -1).reshape(slot_count)
    norm_row = jnp.zeros((1, owners * capacity), jnp.float32).at[0, column].set(piece_norm)
    energy = jnp.sum(light_wide * light_wide)
    current = traces
    background = jnp.zeros((frame_rows,), jnp.float32)
    for pass_index in range(PASSES):
        padded = jnp.concatenate([current, jnp.zeros((frame_rows, 1), jnp.float32)], 1)
        outgoing = jnp.take(padded, lookup, axis=1).astype(jnp.bfloat16)
        incoming = deliver_copies(outgoing)
        copies = jnp.take(incoming, column, axis=1).reshape(frame_rows, cell_count, per_cell)
        modeled = jnp.einsum(
            "ckp,fck->cfp", tile_pieces, copies, preferred_element_type=jnp.float32
        )
        raw_error = tile_movie.astype(jnp.float32) - modeled
        numerator = jnp.sum(light_wide[:, None, :] * raw_error, axis=(0, 2))
        light_total, energy_total = lax.psum((numerator, energy), ("gx", "gy"))
        background = light_total / (energy_total + 1e-06)
        residual = (raw_error - light_wide[:, None, :] * background[None, :, None]).astype(
            jnp.bfloat16
        )
        partials = jnp.einsum(
            "ckp,cfp->fck", tile_pieces, residual, preferred_element_type=jnp.float32
        )
        outbox = (
            jnp.zeros((frame_rows, owners * capacity), jnp.float32)
            .at[:, column]
            .set(partials.reshape(frame_rows, slot_count))
        )
        got_terms, got_norms = deliver_terms(outbox, norm_row)
        summed = jnp.zeros((frame_rows, own_count + 1), jnp.float32).at[:, lookup].add(got_terms)
        weight = jnp.zeros((own_count + 1,), jnp.float32).at[lookup].add(got_norms[0])
        estimate = current + summed[:, :own_count] / jnp.maximum(weight[:own_count], 1.0)
        current = refine(estimate, ar_first, ar_second, mixing)
    return (current, background)


def solution(mesh):
    in_specs = (
        P("gx", "gy", None, "ta", None),
        P("gx", "gy", None, None, None),
        P("gx", "gy", None, None),
        P("gx", "gy", None),
        P("gx", "gy", None, None),
        P("ta", ("gx", "gy")),
        P(("gx", "gy")),
        P(("gx", "gy")),
        P(None, None, ("gx", "gy")),
    )
    out_specs = (P("ta", ("gx", "gy")), P("ta"))
    return jax.shard_map(body, mesh=mesh, in_specs=in_specs, out_specs=out_specs, check_vma=False)
```

profile of v0, /device:TPU:1, one launch (start us, length us, event | category | flops | bytes accessed | tf_op | source)
XLA Modules:
  0.0 1167.2 jit_solution(12223311792273994074)
XLA Ops:
  3.3 8.2 scatter_custom_fusion.5
  12.3 16.3 %all-to-all-start = ((s32[1,128,64]{2,0,1:T(1,128)}), s32[1,128,64]{2,0,1:T(1,128)S(1)}, u32[]{:S(2)}, u32[]{:S(2)}) async-start(s32[1,128,64]{2,0,1:T(1,128)} %bitcast.8), calls=%async_computation | async-start | bytes 131072 | tf_op jit(solution)/shard_map/all_to_all | solution.py:68
  31.9 7.2 all-to-all-done
  39.8 29.2 %gather_fusion = bf16[8192,16]{1,0:T(8,128)(2,1)} fusion(bf16[16,1025]{0,1:T(8,128)(2,1)S(1)} %concatenate.83, s32[8192]{0:T(1024)S(1)} %fusion.42), kind=kCustom, calls=%fused_computation.clone | custom fusion | bytes 557056 | tf_op jit(solution)/shard_map/jit(_take)/gather | solution.py:80
  83.8 8.1 scatter_custom_fusion.6
  95.7 11.7 %all-to-all-start.3 = ((f32[1,128,64]{2,0,1:T(1,128)}), f32[1,128,64]{2,0,1:T(1,128)S(1)}, u32[]{:S(2)}, u32[]{:S(2)}) async-start(f32[1,128,64]{2,0,1:T(1,128)} %bitcast.24), calls=%async_computation.3 | async-start | bytes 131072 | tf_op jit(solution)/shard_map/all_to_all | solution.py:42
  115.3 8.4 multiply_reduce_fusion.2
  123.8 294.8 %all-reduce.27 = (f32[16]{0:T(128)S(1)}, f32[]{:T(128)}) all-reduce(f32[16]{0:T(128)S(1)} %get-tuple-element.16, f32[]{:T(128)} %multiply_reduce_fusion.3), channel_id=1, replica_groups=mesh['gx'=16,'gy'=8,'ta'=2] {'gx','gy'}, use_global_device_ids=true, to_apply=%region_5.8 | all-reduce | flops 17 | bytes 136 | tf_op jit(solution)/shard_map/psum | solution.py:88
  419.3 7.8 fusion.27
  428.4 7.7 scatter_custom_fusion
  448.3 56.0 %scatter_custom_fusion.2 = f32[1025]{0:T(1024)S(1)} fusion(s32[8192]{0:T(1024)S(1)} %bitcast.151, f32[8192]{0:T(1024)S(1)} %reshape.212, f32[]{:T(128)} %constant.28.clone.1), kind=kCustom, calls=%fused_computation.112 | custom fusion | flops 8192 | bytes 4104 | tf_op jit(solution)/shard_map/scatter-add | solution.py:103
  510.3 50.0 %scatter_custom_fusion.1 = f32[16,1025]{0,1:T(8,128)S(1)} fusion(s32[8192]{0:T(1024)S(1)} %bitcast.152, f32[8192,16]{1,0:T(8,128)} %copy.95, f32[]{:T(128)} %constant.28.clone.1), kind=kCustom, calls=%fused_computation.65 | custom fusion | flops 131072 | bytes 66112 | tf_op jit(solution)/shard_map/scatter-add | solution.py:102
  562.4 59.4 %all_gather.6 = f32[32,1024]{1,0:T(8,128)S(1)} all-gather(f32[16,1024]{1,0:T(8,128)S(1)} %divide_add_fusion.1), channel_id=1, replica_groups=mesh['gx'=16,'gy'=8,'ta'=2] {'ta'}, dimensions={0}, use_global_device_ids=true | all-gather | bytes 196608 | tf_op jit(solution)/shard_map/all_gather | solution.py:48
  624.6 29.2 %gather_fusion.2 = bf16[8192,16]{1,0:T(8,128)(2,1)} fusion(bf16[16,1025]{0,1:T(8,128)(2,1)S(1)} %concatenate.96.clone, s32[8192]{0:T(1024)S(1)} %copy-done.5), kind=kCustom, calls=%fused_computation.2.clone | custom fusion | bytes 557056 | tf_op jit(solution)/shard_map/jit(_take)/gather | solution.py:80
  653.8 6.6 bitcast_convert_fusion
  662.6 30.2 %all_to_all.67 = bf16[128,2,512]{2,1,0:T(2,128)(2,1)} all-to-all(bf16[128,2,512]{2,1,0:T(2,128)(2,1)S(1)} %reshape.295), channel_id=1, replica_groups=mesh['gx'=16,'gy'=8,'ta'=2] {'gx','gy'}, dimensions={0} | all-to-all | bytes 524288 | tf_op jit(solution)/shard_map/all_to_all | solution.py:36
  696.0 8.4 gather_fusion.3
  704.8 8.4 multiply_reduce_fusion
  713.2 287.6 %psum.26 = f32[16]{0:T(128)S(1)} all-reduce(f32[16]{0:T(128)S(1)} %get-tuple-element.18), channel_id=1, replica_groups=mesh['gx'=16,'gy'=8,'ta'=2] {'gx','gy'}, use_global_device_ids=true, to_apply=%region_17.20 | all-reduce | flops 16 | bytes 128 | tf_op jit(solution)/shard_map/psum | solution.py:88
  1000.8 7.8 fusion.24
  1009.9 7.9 scatter_custom_fusion.3
  1022.0 21.9 %all_to_all.68 = f32[128,1,1024]{2,1,0:T(1,128)S(1)} all-to-all(f32[128,1,1024]{2,1,0:T(1,128)} %reshape.297), channel_id=1, replica_groups=mesh['gx'=16,'gy'=8,'ta'=2] {'gx','gy'}, dimensions={0} | all-to-all | bytes 1048576 | tf_op jit(solution)/shard_map/all_to_all | solution.py:41
  1053.5 50.0 %scatter_custom_fusion.4 = f32[16,1025]{0,1:T(8,128)S(1)} fusion(s32[8192]{0:T(1024)} %bitcast.153, f32[8192,16]{1,0:T(8,128)} %copy.106, f32[]{:T(128)} %constant.28.clone.1), kind=kCustom, calls=%fused_computation.63 | custom fusion | flops 131072 | bytes 66112 | tf_op jit(solution)/shard_map/scatter-add | solution.py:102
  1103.7 60.1 %all_gather.7 = f32[32,1024]{1,0:T(8,128)S(1)} all-gather(f32[16,1024]{1,0:T(8,128)S(1)} %divide_add_fusion), channel_id=1, replica_groups=mesh['gx'=16,'gy'=8,'ta'=2] {'ta'}, dimensions={0}, use_global_device_ids=true | all-gather | bytes 196608 | tf_op jit(solution)/shard_map/all_gather | solution.py:48
  (153 shorter events, 81.9 us)
Async XLA Ops:
  0.6 2.4 copy-start.19
  0.6 2.5 copy-start.18
  0.7 1.7 copy-start.7
  2.0 29.7 %copy-start.6 = (f32[16,1024]{1,0:T(8,128)S(1)}, f32[16,1024]{1,0:T(8,128)}, u32[]{:S(2)}) copy-start(f32[16,1024]{1,0:T(8,128)} %param.18) | copy-start | bytes 196612
  3.0 105.8 %copy-start.10 = (s32[2048]{0:T(1024)}, s32[2048]{0:T(1024)S(1)}, u32[]{:S(2)}) copy-start(s32[2048]{0:T(1024)S(1)} %get-tuple-element.14) | copy-start | bytes 24580
  3.1 425.3 %copy-start.11 = (s32[2048,1]{0,1:T(1,128)}, s32[2048,1]{0,1:T(1,128)S(1)}, u32[]{:S(2)}) copy-start(s32[2048,1]{0,1:T(1,128)S(1)} %compare_select_fusion.4) | copy-start | bytes 24580
  12.3 26.8 %all-to-all-start = ((s32[1,128,64]{2,0,1:T(1,128)}), s32[1,128,64]{2,0,1:T(1,128)S(1)}, u32[]{:S(2)}, u32[]{:S(2)}) async-start(s32[1,128,64]{2,0,1:T(1,128)} %bitcast.8), calls=%async_computation | async-start | bytes 131072 | tf_op jit(solution)/shard_map/all_to_all | solution.py:68
  39.2 36.6 %copy-start.8 = (pred[8192]{0:T(1024)(128)(4,1)}, pred[8192]{0:T(1024)(128)(4,1)S(1)}, u32[]{:S(2)}) copy-start(pred[8192]{0:T(1024)(128)(4,1)S(1)} %compare_and_fusion) | copy-start | bytes 24580
  39.2 0.6 copy-start.4
  69.0 13.9 %copy-start.1 = (bf16[1,1,128,1024]{3,2,1,0:T(8,128)(2,1)S(1)}, bf16[1,1,128,1024]{3,2,1,0:T(8,128)(2,1)}, u32[]{:S(2)}) copy-start(bf16[1,1,128,1024]{3,2,1,0:T(8,128)(2,1)} %param.17) | copy-start | bytes 786436
  76.8 18.9 %all-to-all-start.1 = ((bf16[128,2,512]{2,1,0:T(2,128)(2,1)}), bf16[128,2,512]{2,1,0:T(2,128)(2,1)S(1)}, u32[]{:S(2)}, u32[]{:S(2)}) async-start(bf16[128,2,512]{2,1,0:T(2,128)(2,1)} %reshape.291), calls=%async_computation.1 | async-start | bytes 524288 | tf_op jit(solution)/shard_map/all_to_all | solution.py:36
  92.7 31.1 %copy-start.15 = (pred[2048]{0:T(1024)(128)(4,1)}, pred[2048]{0:T(1024)(128)(4,1)S(1)}, u32[]{:S(2)}) copy-start(pred[2048]{0:T(1024)(128)(4,1)S(1)} %compare_and_fusion.1) | copy-start | bytes 6148
  95.7 344.7 %all-to-all-start.3 = ((f32[1,128,64]{2,0,1:T(1,128)}), f32[1,128,64]{2,0,1:T(1,128)S(1)}, u32[]{:S(2)}, u32[]{:S(2)}) async-start(f32[1,128,64]{2,0,1:T(1,128)} %bitcast.24), calls=%async_computation.3 | async-start | bytes 131072 | tf_op jit(solution)/shard_map/all_to_all | solution.py:42
  440.4 63.9 %all-to-all-start.2 = ((f32[128,1,1024]{2,1,0:T(1,128)}), f32[128,1,1024]{2,1,0:T(1,128)S(1)}, u32[]{:S(2)}, u32[]{:S(2)}) async-start(f32[128,1,1024]{2,1,0:T(1,128)} %reshape.293), calls=%async_computation.2 | async-start | bytes 1048576 | tf_op jit(solution)/shard_map/all_to_all | solution.py:41
  446.9 63.5 %copy-start.14 = (s32[8192,1]{0,1:T(1,128)}, s32[8192,1]{0,1:T(1,128)S(1)}, u32[]{:S(2)}) copy-start(s32[8192,1]{0,1:T(1,128)S(1)} %compare_select_fusion) | copy-start | bytes 98308
  504.3 58.0 %copy-start.12 = (f32[1024]{0:T(1024)}, f32[1024]{0:T(1024)S(1)}, u32[]{:S(2)}) copy-start(f32[1024]{0:T(1024)S(1)} %slice_maximum_fusion) | copy-start | bytes 12292
  507.4 114.5 %copy-start.2 = (f32[1024]{0:T(1024)S(1)}, f32[1024]{0:T(1024)}, u32[]{:S(2)}) copy-start(f32[1024]{0:T(1024)} %param.20) | copy-start | bytes 12292
  507.4 114.4 %copy-start.3 = (f32[1024]{0:T(1024)S(1)}, f32[1024]{0:T(1024)}, u32[]{:S(2)}) copy-start(f32[1024]{0:T(1024)} %param.19) | copy-start | bytes 12292
  507.7 114.2 %copy-start = (bf16[32,32,1024]{2,1,0:T(8,128)(2,1)S(1)}, bf16[32,32,1024]{2,1,0:T(8,128)(2,1)}, u32[]{:S(2)}) copy-start(bf16[32,32,1024]{2,1,0:T(8,128)(2,1)} %param.21) | copy-start | bytes 6291460
  622.7 1.9 copy-start.5
  623.5 30.3 %copy-start.9 = (pred[8192]{0:T(1024)(128)(4,1)S(1)}, pred[8192]{0:T(1024)(128)(4,1)}, u32[]{:S(2)}) copy-start(pred[8192]{0:T(1024)(128)(4,1)} %copy-done.8) | copy-start | bytes 24580
  660.4 44.0 %copy-start.16 = (pred[2048]{0:T(1024)(128)(4,1)S(1)}, pred[2048]{0:T(1024)(128)(4,1)}, u32[]{:S(2)}) copy-start(pred[2048]{0:T(1024)(128)(4,1)} %copy-done.15) | copy-start | bytes 6148
  1000.8 7.8 copy-start.17
  1049.3 54.3 %copy-start.13 = (f32[1024]{0:T(1024)S(1)}, f32[1024]{0:T(1024)}, u32[]{:S(2)}) copy-start(f32[1024]{0:T(1024)} %copy-done.12) | copy-start | bytes 12292
where the time goes:
time: 1180 us; the launch traced here: 1170 us
  blocking collectives  754 us (64%)
  other arithmetic  185 us (16%)
  local copies, waits for them, and re-layouts  144 us (12%)
  starting transfers between devices  40.6 us (3%)
  matrix products  32.4 us (3%)
    psum x2, blocking collectives, body(): light_total, energy_total = lax.psum((numerator, energy), ('gx', 'gy'))  582 us
    all_gather x2, blocking collectives, refine(): all_frames = lax.all_gather(estimate, 'ta', axis=0, tiled=True)  120 us
    scatter-add x2, other arithmetic, body(): jnp.zeros((frame_rows, own_count + 1), jnp.float32).at[:, lookup]  99.9 us
    gather x2, local copies, waits for them, and re-layouts, body(): outgoing = jnp.take(padded, lookup, axis=1).astype(jnp.bfloat16)  58.4 us
    scatter-add x1, other arithmetic, body(): jnp.zeros((own_count + 1,), jnp.float32).at[lookup].add(got_norms[0])  56 us
    all_to_all x1, blocking collectives, deliver_copies(): lax.all_to_all(outgoing, ('gx', 'gy'), split_axis=1, concat_axis=1, tiled...  30.2 us
    unnamed x54, local copies, waits for them, and re-layouts  26.1 us
  transfers between devices with their start and end apart: 4, of which 2 were waited for; matrix products, arithmetic and copies ran while one was open for 9% of the time, Pallas kernels for 0%

commit v1 on v0

v1 whole, which is shorter than its diff:
```python
import functools
import math

import jax
import jax.numpy as jnp
from jax import lax
from jax.experimental import pallas as pl
from jax.experimental.pallas import tpu as pltpu
from jax.sharding import PartitionSpec as P

DECONV_ITERS = 3
PASSES = 2
CAP = 64
MESH = pl.DeviceIdType.MESH
F32, BF16, I32 = jnp.float32, jnp.bfloat16, jnp.int32


def iota(shape, axis):
    return lax.broadcasted_iota(I32, shape, axis)


def dot(left, right):
    return lax.dot_general(left, right, (((1,), (0,)), ((), ())), preferred_element_type=F32)


def dot_t(left, right):
    return lax.dot_general(left, right, (((1,), (1,)), ((), ())), preferred_element_type=F32)


def split3(value):
    high = value.astype(BF16).astype(F32)
    middle = (value - high).astype(BF16).astype(F32)
    return high, middle, value - high - middle


def kernel(
    dims,
    movie_h, pieces_h, light_h, mixing_h, owner_ref, offset_ref, traces_ref, ar1_ref, ar2_ref,
    out_ref, bg_ref,
    movie, pieces, light, mixing, load_sems,
    slot_m, slot_j, tile_hot, req_out, req_in, owner_hot,
    both_traces, current, current_b,
    block_gram, piece_movie, piece_light, piece_norm, light_movie,
    ext_out, ext_in, dense_ext, dense_ext_in, counts, counts_b, raw_terms,
    rep_out, rep_in, cop, cop_in, terms, num_row, num_row_in,
    spread, send_out, send_in, num_in, gathered, dense, dense_in,
    send_sems, recv_sems,
):
    X, Y, Z, S = dims
    ZH = Z // 2
    M = X * Y * ZH
    MH = M // 2
    NCH = S // 256
    gx, gy, a = lax.axis_index("gx"), lax.axis_index("gy"), lax.axis_index("ta")
    x, y, z = gx // Y, gx % Y, gy
    sibling = (gx, gy, 1 - a)

    def displacement(m):
        dx = (X // 2 + X - m // (Y * ZH)) % X
        dy = (Y // 2 + Y - (m // ZH) % Y) % Y
        dz = 2 * ((ZH // 2 + ZH - m % ZH) % ZH) + (dx + dy + a) % 2
        return dx, dy, dz

    def to_owner(m):
        dx, dy, dz = displacement(m)
        return ((x + dx) % X) * Y + (y + dy) % Y, (z + dz) % Z, a

    def to_tile(m):
        dx, dy, dz = displacement(m)
        return ((x + X - dx) % X) * Y + (y + Y - dy) % Y, (z + Z - dz) % Z, a

    def slot_at(m):
        dx, dy, dz = displacement(m)
        return (((x + X - dx) % X) * Y + (y + Y - dy) % Y) * ZH + ((z + Z - dz) % Z) // 2

    self_m = (X // 2) * Y * ZH + (Y // 2) * ZH + ZH // 2

    def send(source, target, m, peer, sem):
        mine = jnp.logical_and(a == 0, m == self_m)

        @pl.when(mine)
        def _():
            pltpu.make_async_copy(source, target, recv_sems.at[sem]).start()

        @pl.when(jnp.logical_not(mine))
        def _():
            pltpu.make_async_remote_copy(
                source, target, send_sems.at[sem], recv_sems.at[sem], device_id=peer, device_id_type=MESH
            ).start()

    def wait_in(buffer, sem):
        pltpu.make_async_copy(buffer, buffer, recv_sems.at[sem]).wait()

    def wait_out(buffer, sem):
        @pl.when(a == 0)
        def _():
            part = buffer.at[pl.ds(0, M - 1)]
            pltpu.make_async_copy(part, part, send_sems.at[sem]).wait()

        @pl.when(a == 1)
        def _():
            pltpu.make_async_copy(buffer, buffer, send_sems.at[sem]).wait()

    def to_sibling(source, target, sem):
        copy = pltpu.make_async_remote_copy(
            source, target, send_sems.at[sem], recv_sems.at[sem], device_id=sibling, device_id_type=MESH
        )
        copy.start()
        return copy

    loads = []
    rows = movie.shape[0] // 4
    light_load = pltpu.make_async_copy(light_h, light, load_sems.at[8])
    light_load.start()
    for part in range(4):
        span = pl.ds(part * rows, rows)
        pair = (
            pltpu.make_async_copy(pieces_h.at[span], pieces.at[span], load_sems.at[part]),
            pltpu.make_async_copy(movie_h.at[span], movie.at[span], load_sems.at[4 + part]),
        )
        for copy in pair:
            copy.start()
        loads.append(pair)
    mixing_load = pltpu.make_async_copy(mixing_h, mixing, load_sems.at[9])
    mixing_load.start()

    barrier = pltpu.get_barrier_semaphore()

    def greet(m, carry):
        @pl.when(jnp.logical_not(jnp.logical_and(a == 0, m == self_m)))
        def _():
            pl.semaphore_signal(barrier, inc=1, device_id=to_owner(m), device_id_type=MESH)

        return carry

    pl.semaphore_signal(barrier, inc=1, device_id=sibling, device_id_type=MESH)
    lax.fori_loop(0, M, greet, 0)

    own_of = owner_ref[...]
    far = own_of // Z
    rel_x = (far // Y - x) & (X - 1)
    rel_y = (far % Y - y) & (Y - 1)
    rel_z = (own_of % Z - z) & (Z - 1)
    parity = (rel_x + rel_y + rel_z) & 1
    partner = (
        ((X // 2 - rel_x) & (X - 1)) * (Y * ZH)
        + ((Y // 2 - rel_y) & (Y - 1)) * ZH
        + ((ZH // 2 - (rel_z >> 1)) & (ZH - 1))
    )
    partner = jnp.where(parity == a, partner, -1)
    before = jnp.where(iota((256, 256), 0) < iota((256, 256), 1), 1.0, 0.0).astype(BF16)
    base = jnp.zeros((M, 1), F32)
    asked = jnp.zeros((2 * M, 2 * CAP), F32)
    place1 = offset_ref[...] + 1
    for chunk in range(NCH):
        lanes = slice(chunk * 256, chunk * 256 + 256)
        who = partner[:, lanes]
        match = iota((M, 256), 0) == who
        match_f = jnp.where(match, 1.0, 0.0)
        count = dot(match_f.astype(BF16), before) + base
        rank = jnp.sum(match_f * count, axis=0, keepdims=True).astype(I32)
        base = base + jnp.sum(match_f, axis=1, keepdims=True)
        slot_m[chunk] = who
        slot_j[chunk] = rank
        wanted = place1[:, lanes]
        halves = jnp.concatenate(
            [
                jnp.where(match, (wanted >> 5).astype(F32), 0.0),
                jnp.where(match, (wanted & 31).astype(F32), 0.0),
            ],
            axis=0,
        ).astype(BF16)
        where_to = jnp.where((iota((2 * CAP, 256), 0) & (CAP - 1)) == rank, 1.0, 0.0).astype(BF16)
        asked = asked + dot_t(halves, where_to)
    req_out[...] = ((asked[:M] * 32.0 + asked[M:]).astype(I32) - 1).reshape(M, 1, 2 * CAP)

    pl.semaphore_wait(barrier, M + a)
    both_traces[a] = traces_ref[...]
    trace_copy = to_sibling(both_traces.at[a], both_traces.at[a], 0)

    def ask(m, carry):
        send(req_out.at[m], req_in.at[m], m, to_owner(m), 1)
        return carry

    lax.fori_loop(0, M, ask, 0)

    def tile_maps(chunk, carry):
        who, rank = slot_m[chunk], slot_j[chunk]
        upper = (who >= MH).astype(I32)
        lanes = pl.ds(pl.multiple_of(chunk * 256, 256), 256)
        for half in range(2):
            row = jnp.where(who >= 0, upper * 128 + half * CAP + rank, -1)
            tile_hot[half, :, lanes] = jnp.where(iota((256, 256), 0) == row, 1.0, 0.0).astype(BF16)
        return carry

    lax.fori_loop(0, NCH, tile_maps, 0)

    light_load.wait()
    same_cell = (iota((256, 256), 0) >> 4) == (iota((256, 256), 1) >> 4)
    diagonal = iota((256, 256), 0) == iota((256, 256), 1)
    light_cell = iota((16, 256), 0) == (iota((16, 256), 1) >> 4)
    movie_cell = (iota((256, 16), 0) >> 4) == iota((256, 16), 1)

    def gram(chunk, carry):
        numer, energy = carry
        span = pl.ds(pl.multiple_of(chunk * 256, 256), 256)
        block, frames = pieces[span, :], movie[span, :]
        lit = light[pl.ds(pl.multiple_of(chunk * 16, 16), 16), :]
        cross = jnp.where(same_cell, dot_t(frames, block), 0.0)
        piece_movie[chunk] = jnp.sum(cross.reshape(16, 16, 256), axis=0)
        square = jnp.where(same_cell, dot_t(block, block), 0.0)
        high = square.astype(BF16)
        block_gram[0, chunk] = high
        block_gram[1, chunk] = (square - high.astype(F32)).astype(BF16)
        piece_norm[chunk] = jnp.sum(jnp.where(diagonal, square, 0.0), axis=0, keepdims=True)
        piece_light[chunk] = jnp.sum(jnp.where(light_cell, dot_t(lit, block), 0.0), axis=0, keepdims=True)
        shine = jnp.where(movie_cell, dot_t(frames, lit), 0.0)
        numer = numer + jnp.sum(shine.reshape(16, 16, 16), axis=0)
        lit_f = lit.astype(F32)
        return numer, energy + lit_f * lit_f

    carry = (jnp.zeros((16, 16), F32), jnp.zeros((16, 1024), F32))
    for part in range(4):
        for copy in loads[part]:
            copy.wait()
        carry = lax.fori_loop(part * NCH // 4, (part + 1) * NCH // 4, gram, carry)
    light_movie[...] = jnp.sum(carry[0], axis=1, keepdims=True)
    energy = jnp.sum(jnp.sum(carry[1], axis=1, keepdims=True), axis=0, keepdims=True)

    trace_copy.wait()
    for q in range(4):
        lanes = slice(q * 256, q * 256 + 256)
        for half in range(2):
            part = both_traces[half, :, lanes]
            current[q, half] = part
            current_b[half, q] = part.astype(BF16)
    wait_in(req_in, 1)

    def answer(build, number):
        right = (iota((1, 256), 1) & (2 * CAP - 1)) >= CAP

        def pair(i, carry):
            index = jnp.concatenate([req_in[2 * i], req_in[2 * i + 1]], axis=1)
            lanes = pl.ds(pl.multiple_of(i * 256, 256), 256)
            if build:
                hot = jnp.where(iota((256, 256), 0) == (index & 255), 1.0, 0.0).astype(BF16)
                owner_hot[:, lanes] = hot
            else:
                hot = owner_hot[:, lanes]
            found = dot(current_b[...].reshape(128, 256), hot).reshape(2, 4, 16, 256)
            group = index >> 8
            total = jnp.zeros((16, 256), F32)
            for q in range(4):
                total = total + jnp.where(group == q, jnp.where(right, found[1, q], found[0, q]), 0.0)
            total = total.astype(BF16)
            for side in range(2):
                m = 2 * i + side
                rep_out[number, m] = total[:, side * 128 : side * 128 + 128]
                send(rep_out.at[number, m], rep_in.at[number, m], m, to_tile(m), 2 + number)
            return carry

        lax.fori_loop(0, MH, pair, 0)

    def extras():
        total = jnp.zeros((M, 2 * CAP), F32)
        for chunk in range(NCH):
            who, rank = slot_m[chunk], slot_j[chunk]
            match = iota((M, 256), 0) == who
            for half, value in ((0, piece_norm[chunk]), (1, piece_light[chunk])):
                spot = jnp.where(iota((2 * CAP, 256), 0) == half * CAP + rank, 1.0, 0.0).astype(BF16)
                for piece in split3(value):
                    total = total + dot_t(jnp.where(match, piece, 0.0).astype(BF16), spot)
        ext_out[...] = total.reshape(M, 1, 2 * CAP)

        def post(m, carry):
            send(ext_out.at[m], ext_in.at[m], m, to_owner(m), 4)
            return carry

        lax.fori_loop(0, M, post, 0)

    def collect_extras():
        row, lane = iota((32, 256), 0), iota((32, 256), 1)
        part, group = row >> 3, row & 3
        right = ((lane & (2 * CAP - 1)) >= CAP).astype(I32)
        wanted = jnp.logical_or(
            jnp.logical_and(part < 3, ((row >> 2) & 1) == right),
            jnp.logical_and(part == 3, jnp.logical_and(right == 0, ((row >> 2) & 1) == (lane >> 7))),
        )
        wanted = jnp.where(wanted, group, -2)

        def pair(i, carry):
            index = jnp.concatenate([req_in[2 * i], req_in[2 * i + 1]], axis=1)
            value = jnp.concatenate([ext_in[2 * i], ext_in[2 * i + 1]], axis=1)
            high, middle, low = split3(value)
            picked = jnp.where(part == 0, high, jnp.where(part == 1, middle, jnp.where(part == 2, low, 1.0)))
            keep = wanted == (index >> 8)
            lanes = pl.ds(pl.multiple_of(i * 256, 256), 256)
            found = dot_t(jnp.where(keep, picked, 0.0).astype(BF16), owner_hot[:, lanes])
            counts[slot_at(2 * i)] = found[24:28]
            counts[slot_at(2 * i + 1)] = found[28:32]
            return carry + found

        dense_ext[...] = lax.fori_loop(0, MH, pair, jnp.zeros((32, 256), F32))
        for q in range(4):
            counts_b[q] = counts[:, q, :].astype(BF16)

    pending = []
    for number in range(PASSES):
        answer(number == 0, number)
        if number == 0:
            extras()
        wait_in(rep_in.at[number], 2 + number)

        def pick(half):
            def chunk_of(chunk, carry):
                lanes = pl.ds(pl.multiple_of(chunk * 256, 256), 256)
                low = rep_in[number, :MH].reshape(MH * 16, 128)
                top = rep_in[number, MH:].reshape(MH * 16, 128)
                found = dot(jnp.concatenate([low, top], axis=1), tile_hot[half, :, lanes])
                who = slot_m[chunk]
                who = jnp.where(who >= MH, who - MH, who)
                found = found.reshape(MH, 16, 256)
                kept = jnp.where(iota((MH, 16, 256), 0) == who.reshape(1, 1, 256), found, 0.0)
                cop[number, half, chunk] = jnp.sum(kept, axis=0).astype(BF16)
                return carry

            lax.fori_loop(0, NCH, chunk_of, 0)

        pick(1 - a)
        copy = to_sibling(cop.at[number, 1 - a], cop_in.at[number], 5 + number)
        pick(a)
        copy.wait_recv()
        pending.append(copy)

        def term(chunk, carry):
            copies = cop[number, a, chunk] + cop_in[number, chunk]
            model = dot(copies, block_gram[0, chunk]) + dot(copies, block_gram[1, chunk])
            raw = piece_movie[chunk] - model
            raw_terms[chunk] = raw
            return carry[0] + piece_light[chunk] * copies.astype(F32), carry[1] + raw

        lit, level = lax.fori_loop(0, NCH, term, (jnp.zeros((16, 256), F32), jnp.zeros((16, 256), F32)))
        level = (jnp.sum(level, axis=1, keepdims=True) * (1.0 / S)).astype(BF16).astype(F32)
        for chunk in range(NCH):
            terms[number, a, chunk] = (raw_terms[chunk] - level).astype(BF16)
        copy = to_sibling(terms.at[number, a], terms.at[number, a], 7 + number)
        pending.append(copy)
        numer = light_movie[...] - jnp.sum(lit, axis=1, keepdims=True)
        spot = iota((16, 128), 1) == iota((16, 128), 0) + 16 * a
        level_spot = iota((16, 128), 1) == iota((16, 128), 0) + 16 * a + 64
        numer = jnp.where(spot, numer, jnp.where(level_spot, level, 0.0))
        numer = jnp.sum(numer, axis=0, keepdims=True)
        numer = numer + jnp.where(jnp.logical_and(iota((1, 128), 1) == 32, a == 0), energy, 0.0)
        num_row[number, a] = numer
        row_copy = to_sibling(num_row.at[number, a], num_row.at[number, a], 9 + number)
        pending.append(row_copy)

        def scatter(half):
            def fill(chunk, carry):
                lanes = pl.ds(pl.multiple_of(chunk * 256, 256), 256)
                who = slot_m[chunk]
                who = jnp.where(who >= MH, who - MH, who)
                value = terms[number, half, chunk].astype(F32)
                mask = iota((MH, 16, 256), 0) == who.reshape(1, 1, 256)
                kept = jnp.where(mask, value.reshape(1, 16, 256), 0.0)
                spread[:, lanes] = kept.reshape(MH * 16, 256).astype(BF16)
                return carry

            lax.fori_loop(0, NCH, fill, 0)
            return dot_t(spread[...], tile_hot[half])

        first = scatter(a)
        copy.wait_recv()
        total = (first + scatter(1 - a)).astype(BF16)
        send_out[number, :MH] = total[:, :128].reshape(MH, 16, 128)
        send_out[number, MH:] = total[:, 128:].reshape(MH, 16, 128)
        row_copy.wait_recv()
        num_row_in[number] = num_row[number, 0] + num_row[number, 1]
        tile_parity = (x + y + z) % 2
        tile_slot = tile_parity * M + (x * Y + y) * ZH + z // 2

        def post(m, carry):
            send(send_out.at[number, m], send_in.at[number, m], m, to_owner(m), 11 + number)
            send(num_row_in.at[number], num_in.at[number, tile_slot], m, to_owner(m), 13 + number)
            return carry

        lax.fori_loop(0, M, post, 0)

        if number == 0:
            wait_in(ext_in, 4)
            collect_extras()
            ext_copy = to_sibling(dense_ext, dense_ext_in, 15)
            pending.append(ext_copy)
            mixing_load.wait()

        half_at = ((x + y + z + a) % 2) * M
        mine = num_in.at[number, pl.ds(half_at, M)]
        wait_in(mine, 13 + number)
        num_copy = to_sibling(mine, mine, 16 + number)
        pending.append(num_copy)

        wait_in(send_in.at[number], 11 + number)
        right = (iota((1, 256), 1) & (2 * CAP - 1)) >= CAP

        def gather_rows(i, carry):
            index = jnp.concatenate([req_in[2 * i], req_in[2 * i + 1]], axis=1)
            value = jnp.concatenate([send_in[number, 2 * i], send_in[number, 2 * i + 1]], axis=1).astype(F32)
            group = index >> 8
            lanes = pl.ds(pl.multiple_of(i * 256, 256), 256)
            for half in range(2):
                for q in range(4):
                    keep = jnp.logical_and(group == q, right if half else jnp.logical_not(right))
                    at = (half * 4 + q) * 16
                    gathered[at : at + 16, lanes] = jnp.where(keep, value, 0.0).astype(BF16)
            return carry

        lax.fori_loop(0, MH, gather_rows, 0)
        sums = dot_t(gathered[...], owner_hot[...]).reshape(2, 4, 16, 256)
        levels = jnp.transpose(mine[...].reshape(M, 128))[64:96].astype(BF16)
        for q in range(4):
            dense[number, :, q] = sums[:, q] + dot(levels, counts_b[q]).reshape(2, 16, 256)
        dense_copy = to_sibling(dense.at[number], dense_in.at[number], 18 + number)
        pending.append(dense_copy)
        if number == 0:
            ext_copy.wait_recv()
        num_copy.wait_recv()
        totals = jnp.sum(num_in[number], axis=0)
        light_energy = jnp.sum(jnp.where(iota((1, 128), 1) == 32, totals, 0.0), axis=1, keepdims=True)
        bg_row = totals / (light_energy + 1e-6)
        bg = jnp.sum(jnp.where(iota((32, 128), 1) == iota((32, 128), 0), bg_row, 0.0), axis=1, keepdims=True)
        dense_copy.wait_recv()
        frame = iota((32, 256), 0)

        def back(values, lag):
            return jnp.where(frame >= lag, pltpu.roll(values, lag, 0), 0.0)

        def ahead(values, lag):
            return jnp.where(frame < 32 - lag, pltpu.roll(values, 32 - lag, 0), 0.0)

        for q in range(4):
            lanes = slice(q * 256, q * 256 + 256)
            ext = dense_ext[...] + dense_ext_in[...]
            weight = ext[q : q + 1] + ext[8 + q : 9 + q] + ext[16 + q : 17 + q]
            shine = ext[4 + q : 5 + q] + ext[12 + q : 13 + q] + ext[20 + q : 21 + q]
            summed = (dense[number, :, q] + dense_in[number, :, q]).reshape(32, 256) - bg * shine
            target = current[q].reshape(32, 256) + summed / jnp.maximum(weight, 1.0)
            g1, g2 = ar1_ref[:, lanes], ar2_ref[:, lanes]
            latest = target
            dual = jnp.zeros_like(target)
            for sweep in range(DECONV_ITERS):
                filtered = latest - g1 * back(latest, 1) - g2 * back(latest, 2)
                spikes = jnp.maximum(filtered + dual, 0.0)
                dual = dual + filtered - spikes
                drive = spikes - dual
                drive = target + (drive - g1 * ahead(drive, 1) - g2 * ahead(drive, 2))
                parts = []
                for block in range(4):
                    matrix = mixing[block * 256 : block * 256 + 256, lanes].astype(F32).reshape(8, 32, 256)
                    parts.append(jnp.sum(matrix * drive.reshape(1, 32, 256), axis=1))
                latest = jnp.concatenate(parts, axis=0)
            latest = latest.reshape(2, 16, 256)
            current[q] = latest
            if number < PASSES - 1:
                current_b[:, q] = latest.astype(BF16)
        if number == PASSES - 1:
            for q in range(4):
                out_ref[:, q * 256 : q * 256 + 256] = current[q, a]
            own = iota((32, 128), 0) == iota((32, 128), 1) + 16 * a
            bg_ref[...] = jnp.sum(jnp.where(own, bg, 0.0), axis=0, keepdims=True)

    for copy in pending:
        copy.wait_send()
    wait_out(req_in, 1)
    wait_out(ext_in, 4)
    for number in range(PASSES):
        wait_out(rep_in.at[number], 2 + number)
        wait_out(send_in.at[number], 11 + number)
        wait_out(num_in.at[number, pl.ds(0, M)], 13 + number)


def solution(mesh):
    along_x, Z = mesh.shape["gx"], mesh.shape["gy"]
    X = math.isqrt(along_x)
    Y = along_x // X

    def body(movie, pieces, owner, block_offset, light, traces, ar_first, ar_second, mixing):
        cells, frames, pixels = movie.shape[2], movie.shape[3], movie.shape[4]
        S = cells * pieces.shape[3]
        M = X * Y * Z // 2
        NCH = S // 256
        own = traces.shape[1]
        any_spec = pl.BlockSpec(memory_space=pl.ANY)
        vmem_spec = pl.BlockSpec(memory_space=pltpu.VMEM)
        V = pltpu.VMEM
        scratch = [
            V((cells * frames, pixels), BF16), V((S, pixels), BF16), V((cells, pixels), BF16),
            V((1024, own), BF16), pltpu.SemaphoreType.DMA((10,)),
            V((NCH, 1, 256), I32), V((NCH, 1, 256), I32), V((2, 256, S), BF16),
            V((M, 1, 128), I32), V((M, 1, 128), I32), V((256, M * 128), BF16),
            V((2, 16, own), F32), V((4, 2, 16, 256), F32), V((2, 4, 16, 256), BF16),
            V((2, NCH, 256, 256), BF16), V((NCH, 16, 256), F32), V((NCH, 1, 256), F32),
            V((NCH, 1, 256), F32), V((16, 1), F32),
            V((M, 1, 128), F32), V((M, 1, 128), F32), V((32, 256), F32), V((32, 256), F32),
            V((M, 4, 256), F32), V((4, M, 256), BF16), V((NCH, 16, 256), F32),
            V((PASSES, M, 16, 128), BF16), V((PASSES, M, 16, 128), BF16),
            V((PASSES, 2, NCH, 16, 256), BF16), V((PASSES, NCH, 16, 256), BF16),
            V((PASSES, 2, NCH, 16, 256), BF16),
            V((PASSES, 2, 1, 128), F32), V((PASSES, 1, 128), F32),
            V((M * 8, S), BF16), V((PASSES, M, 16, 128), BF16), V((PASSES, M, 16, 128), BF16),
            V((PASSES, 2 * M, 1, 128), F32), V((128, M * 128), BF16),
            V((PASSES, 2, 4, 16, 256), F32), V((PASSES, 2, 4, 16, 256), F32),
            pltpu.SemaphoreType.DMA((20,)), pltpu.SemaphoreType.DMA((20,)),
        ]
        result, background = pl.pallas_call(
            functools.partial(kernel, (X, Y, Z, S)),
            out_shape=(
                jax.ShapeDtypeStruct((frames, own), F32),
                jax.ShapeDtypeStruct((1, 128), F32),
            ),
            in_specs=[any_spec] * 4 + [vmem_spec] * 5,
            out_specs=(vmem_spec, vmem_spec),
            scratch_shapes=scratch,
            compiler_params=pltpu.CompilerParams(
                collective_id=0, has_side_effects=True, vmem_limit_bytes=56 * 1024 * 1024
            ),
            name="cnmf_passes",
        )(
            movie.reshape(cells * frames, pixels),
            pieces.reshape(S, pixels),
            light.reshape(cells, pixels),
            mixing.reshape(1024, own),
            owner.reshape(1, S),
            block_offset.reshape(1, S),
            traces,
            ar_first.reshape(1, own),
            ar_second.reshape(1, own),
        )
        return result, background[0, :frames]

    in_specs = (
        P("gx", "gy", None, "ta", None),
        P("gx", "gy", None, None, None),
        P("gx", "gy", None, None),
        P("gx", "gy", None),
        P("gx", "gy", None, None),
        P("ta", ("gx", "gy")),
        P(("gx", "gy")),
        P(("gx", "gy")),
        P(None, None, ("gx", "gy")),
    )
    out_specs = (P("ta", ("gx", "gy")), P("ta"))
    return jax.shard_map(body, mesh=mesh, in_specs=in_specs, out_specs=out_specs, check_vma=False)
```

time: 1180 us -> 104 us (0.09); the launches traced: 1170 us -> 104 us
  blocking collectives: 754 us -> 0 us
  other arithmetic: 185 us -> 0 us
  local copies, waits for them, and re-layouts: 144 us -> 2.59 us
  Pallas kernels: 0 us -> 100 us
  starting transfers between devices: 40.6 us -> 0 us
  matrix products: 32.4 us -> 0 us
    psum x2 -> x0, blocking collectives: 582 us -> none  [body(): light_total, energy_total = lax.psum((numerator, energy), ('gx', 'gy'))]
    scatter-add x3 -> x0, other arithmetic: 156 us -> none  [the longest x2 99.9 us: body(): jnp.zeros((frame_rows, own_count + 1), jnp.float32).at[:, lookup]]
    all_gather x2 -> x0, blocking collectives: 120 us -> none  [refine(): all_frames = lax.all_gather(estimate, 'ta', axis=0, tiled=True)]
    pallas_call x0 -> x1, Pallas kernels: none -> 100 us  [body(): pl.pallas_call(functools.partial(kernel, (X, Y, Z, S)), out_shape=(jax.Sh...]
    gather x4 -> x0, local copies, waits for them, and re-layouts: 73.1 us -> none  [the longest x2 58.4 us: body(): outgoing = jnp.take(padded, lookup, axis=1).astype(jnp.bfloat16)]
    all_to_all x2 -> x0, blocking collectives: 52.1 us -> none  [the longest x1 30.2 us: deliver_copies(): lax.all_to_all(outgoing, ('gx', 'gy'), split_axis=1, concat_axis=1, tiled...]
    all_to_all x4 -> x0, starting transfers between devices: 40.6 us -> none  [the longest x1 16.3 us: body(): lax.all_to_all(request, ('gx', 'gy'), split_axis=1, concat_axis=1, tiled=...]
    dot_general x4 -> x0, matrix products: 32.4 us -> none  [the longest x2 16.9 us: body(): jnp.einsum('ckp,fck->cfp', tile_pieces, copies, preferred_element_type=jn...]
  transfers between devices with their start and end apart: 4 -> 0, of which waited for: 2 -> 0; matrix products, arithmetic and copies ran while one was open for 9% -> 0% of each run, Pallas kernels for 0% -> 0%
where the time goes in v1:
time: 104 us
  Pallas kernels  100 us (96%)
  local copies, waits for them, and re-layouts  2.59 us (2%)
    pallas_call x1, Pallas kernels, body(): pl.pallas_call(functools.partial(kernel, (X, Y, Z, S)), out_shape=(jax.Sh...  100 us

profile of v1, /device:TPU:1, one launch (start us, length us, event | category | flops | bytes accessed | tf_op | source)
XLA Modules:
  0.0 103.7 jit_solution(8461932478475768162)
XLA Ops:
  0.6 100.4 %cnmf_passes.1 = (f32[16,1024]{1,0:T(8,128)}, f32[1,128]{1,0:T(1,128)}) custom-call(bf16[2048,1024]{1,0:T(8,128)(2,1)} %bitcast.10, bf16[2048,1024]{1,0:T(8,128)(2,1)} %bitcast.11, bf16[128,1024]{1,0:T(8,128)(2,1)} %bitcast.13, bf16[1024,1024]{1,0:T(8,128)(2,1)} %bitcast.12, s32[1,2048]{1,0:T(1,128)} %bitcast.14, s32[1,2048]{1,0:T(1,128)} %bitcast.15, ...), custom_call_target="tpu_custom_call" | custom-call | tf_op jit(solution)/shard_map/cnmf_passes/pallas_call | solution.py:514
  101.1 1.1 %slice_bitcast_fusion = f32[16]{0:T(128)} fusion(f32[1,128]{1,0:T(1,128)} %get-tuple-element.5), kind=kLoop, calls=%fused_computation | loop fusion | bytes 128 | tf_op jit(solution)/shard_map/squeeze | solution.py:538
  102.2 1.5 %copy.12 = f32[16,1024]{1,0:T(8,128)} copy(f32[16,1024]{1,0:T(8,128)} %get-tuple-element.8) | data formatting | bytes 131072

commit v2 on v1

--- a/solution.py
+++ b/solution.py
@@ -38,28 +38,37 @@
     movie_h, pieces_h, light_h, mixing_h, owner_ref, offset_ref, traces_ref, ar1_ref, ar2_ref,
     out_ref, bg_ref,
     movie, pieces, light, mixing, load_sems,
-    slot_m, slot_j, tile_hot, req_out, req_in, owner_hot,
+    slot_m, slot_j, tile_hot, req_out, req_in, owner_hot, owner_row,
     both_traces, current, current_b,
     block_gram, piece_movie, piece_light, piece_norm, light_movie,
     ext_out, ext_in, dense_ext, dense_ext_in, counts, counts_b, raw_terms,
-    rep_out, rep_in, cop, cop_in, terms, num_row, num_row_in,
-    spread, send_out, send_in, num_in, gathered, dense, dense_in,
+    rep_out, rep_in, unpacked, cop, cop_in, terms, num_row, num_row_in,
+    spread, packed, send_out, send_in, num_in, gathered, dense, dense_in,
     send_sems, recv_sems,
 ):
     X, Y, Z, S = dims
     ZH = Z // 2
     M = X * Y * ZH
-    MH = M // 2
+    G = M // 4
+    PART = M // 4
     NCH = S // 256
     gx, gy, a = lax.axis_index("gx"), lax.axis_index("gy"), lax.axis_index("ta")
     x, y, z = gx // Y, gx % Y, gy
     sibling = (gx, gy, 1 - a)
 
+    def hops(place):
+        dx, dy, half_dz = place
+        along_z = sum(min(2 * half_dz + odd, Z - 2 * half_dz - odd) for odd in (0, 1))
+        return 2 * min(dx, X - dx) + 2 * min(dy, Y - dy) + along_z
+
+    places = [(i // (Y * ZH), (i // ZH) % Y, i % ZH) for i in range(M)]
+    order = sorted(range(M), key=lambda i: (-hops(places[i]), i))
+    number_of = [order.index(i) for i in range(M)]
+    self_m = number_of[0]
+
     def displacement(m):
-        dx = (X // 2 + X - m // (Y * ZH)) % X
-        dy = (Y // 2 + Y - (m // ZH) % Y) % Y
-        dz = 2 * ((ZH // 2 + ZH - m % ZH) % ZH) + (dx + dy + a) % 2
-        return dx, dy, dz
+        dx, dy, half_dz = places[order[m]]
+        return dx, dy, 2 * half_dz + (dx + dy + a) % 2
 
     def to_owner(m):
         dx, dy, dz = displacement(m)
@@ -73,20 +82,40 @@
         dx, dy, dz = displacement(m)
         return (((x + X - dx) % X) * Y + (y + Y - dy) % Y) * ZH + ((z + Z - dz) % Z) // 2
 
-    self_m = (X // 2) * Y * ZH + (Y // 2) * ZH + ZH // 2
-
-    def send(source, target, m, peer, sem):
-        mine = jnp.logical_and(a == 0, m == self_m)
-
-        @pl.when(mine)
+    def send(source, target, m, peer, sem, recv=None):
+        recv = sem if recv is None else recv
+        remote = pltpu.make_async_remote_copy(
+            source, target, send_sems.at[sem], recv_sems.at[recv], device_id=peer, device_id_type=MESH
+        )
+        if m != self_m:
+            remote.start()
+            return
+
+        @pl.when(a == 0)
         def _():
-            pltpu.make_async_copy(source, target, recv_sems.at[sem]).start()
-
-        @pl.when(jnp.logical_not(mine))
+            pltpu.make_async_copy(source, target, recv_sems.at[recv]).start()
+
+        @pl.when(a == 1)
         def _():
-            pltpu.make_async_remote_copy(
-                source, target, send_sems.at[sem], recv_sems.at[sem], device_id=peer, device_id_type=MESH
-            ).start()
+            remote.start()
+
+    left = iota((1, 2 * CAP), 1) < CAP
+
+    def swap_halves(first, second):
+        return (
+            jnp.where(left, first, pltpu.roll(second, CAP, 1)),
+            jnp.where(left, pltpu.roll(first, CAP, 1), second),
+        )
+
+    def unpack4(ref, g):
+        tiles = [ref[4 * g + side].astype(F32) for side in range(4)]
+        low, high = swap_halves(tiles[0], tiles[1]), swap_halves(tiles[2], tiles[3])
+        return [jnp.concatenate([low[half], high[half]], axis=1) for half in range(2)]
+
+    def pack4(first, second):
+        low = swap_halves(first[:, :128], second[:, :128])
+        high = swap_halves(first[:, 128:], second[:, 128:])
+        return low + high
 
     def wait_in(buffer, sem):
         pltpu.make_async_copy(buffer, buffer, recv_sems.at[sem]).wait()
@@ -126,15 +155,14 @@
 
     barrier = pltpu.get_barrier_semaphore()
 
-    def greet(m, carry):
-        @pl.when(jnp.logical_not(jnp.logical_and(a == 0, m == self_m)))
-        def _():
+    pl.semaphore_signal(barrier, inc=1, device_id=sibling, device_id_type=MESH)
+    for m in range(M):
+        if m != self_m:
             pl.semaphore_signal(barrier, inc=1, device_id=to_owner(m), device_id_type=MESH)
 
-        return carry
-
-    pl.semaphore_signal(barrier, inc=1, device_id=sibling, device_id_type=MESH)
-    lax.fori_loop(0, M, greet, 0)
+    @pl.when(a == 1)
+    def _():
+        pl.semaphore_signal(barrier, inc=1, device_id=to_owner(self_m), device_id_type=MESH)
 
     own_of = owner_ref[...]
     far = own_of // Z
@@ -142,11 +170,12 @@
     rel_y = (far % Y - y) & (Y - 1)
     rel_z = (own_of % Z - z) & (Z - 1)
     parity = (rel_x + rel_y + rel_z) & 1
-    partner = (
-        ((X // 2 - rel_x) & (X - 1)) * (Y * ZH)
-        + ((Y // 2 - rel_y) & (Y - 1)) * ZH
-        + ((ZH // 2 - (rel_z >> 1)) & (ZH - 1))
-    )
+    key = (rel_x * Y + rel_y) * ZH + (rel_z >> 1)
+    packed_numbers = jnp.zeros_like(key)
+    for word in range(M // 4):
+        value = sum(number_of[4 * word + byte] << (8 * byte) for byte in range(4))
+        packed_numbers = jnp.where((key >> 2) == word, value, packed_numbers)
+    partner = (packed_numbers >> ((key & 3) * 8)) & 255
     partner = jnp.where(parity == a, partner, -1)
     before = jnp.where(iota((256, 256), 0) < iota((256, 256), 1), 1.0, 0.0).astype(BF16)
     base = jnp.zeros((M, 1), F32)
@@ -178,22 +207,17 @@
     both_traces[a] = traces_ref[...]
     trace_copy = to_sibling(both_traces.at[a], both_traces.at[a], 0)
 
-    def ask(m, carry):
+    for m in range(M):
         send(req_out.at[m], req_in.at[m], m, to_owner(m), 1)
-        return carry
-
-    lax.fori_loop(0, M, ask, 0)
 
     def tile_maps(chunk, carry):
         who, rank = slot_m[chunk], slot_j[chunk]
-        upper = (who >= MH).astype(I32)
         lanes = pl.ds(pl.multiple_of(chunk * 256, 256), 256)
-        for half in range(2):
-            row = jnp.where(who >= 0, upper * 128 + half * CAP + rank, -1)
-            tile_hot[half, :, lanes] = jnp.where(iota((256, 256), 0) == row, 1.0, 0.0).astype(BF16)
+        row = jnp.where(who >= 0, (who & 3) * CAP + rank, -1)
+        tile_hot[:, lanes] = jnp.where(iota((256, 256), 0) == row, 1.0, 0.0).astype(BF16)
         return carry
 
-    lax.fori_loop(0, NCH, tile_maps, 0)
+    lax.fori_loop(0, NCH, tile_maps, 0, unroll=2)
 
     light_load.wait()
     same_cell = (iota((256, 256), 0) >> 4) == (iota((256, 256), 1) >> 4)
@@ -223,7 +247,7 @@
     for part in range(4):
         for copy in loads[part]:
             copy.wait()
-        carry = lax.fori_loop(part * NCH // 4, (part + 1) * NCH // 4, gram, carry)
+        carry = lax.fori_loop(part * NCH // 4, (part + 1) * NCH // 4, gram, carry, unroll=2)
     light_movie[...] = jnp.sum(carry[0], axis=1, keepdims=True)
     energy = jnp.sum(jnp.sum(carry[1], axis=1, keepdims=True), axis=0, keepdims=True)
 
@@ -237,29 +261,33 @@
     wait_in(req_in, 1)
 
     def answer(build, number):
-        right = (iota((1, 256), 1) & (2 * CAP - 1)) >= CAP
-
-        def pair(i, carry):
-            index = jnp.concatenate([req_in[2 * i], req_in[2 * i + 1]], axis=1)
-            lanes = pl.ds(pl.multiple_of(i * 256, 256), 256)
+        for g in range(G):
+            lanes = slice(g * 256, g * 256 + 256)
             if build:
+                asked_for = [req_in[4 * g + side] for side in range(4)]
+                index = jnp.concatenate(
+                    [jnp.where(left, asked_for[0], asked_for[1]), jnp.where(left, asked_for[2], asked_for[3])], axis=1
+                )
+                owner_row[g] = index
                 hot = jnp.where(iota((256, 256), 0) == (index & 255), 1.0, 0.0).astype(BF16)
                 owner_hot[:, lanes] = hot
             else:
+                index = owner_row[g]
                 hot = owner_hot[:, lanes]
             found = dot(current_b[...].reshape(128, 256), hot).reshape(2, 4, 16, 256)
-            group = index >> 8
-            total = jnp.zeros((16, 256), F32)
+            block = index >> 8
+            totals = [jnp.zeros((16, 256), F32), jnp.zeros((16, 256), F32)]
             for q in range(4):
-                total = total + jnp.where(group == q, jnp.where(right, found[1, q], found[0, q]), 0.0)
-            total = total.astype(BF16)
-            for side in range(2):
-                m = 2 * i + side
-                rep_out[number, m] = total[:, side * 128 : side * 128 + 128]
-                send(rep_out.at[number, m], rep_in.at[number, m], m, to_tile(m), 2 + number)
-            return carry
-
-        lax.fori_loop(0, MH, pair, 0)
+                keep = block == q
+                for half in range(2):
+                    totals[half] = totals[half] + jnp.where(keep, found[half, q], 0.0)
+            for side, tile in enumerate(pack4(*totals)):
+                m = 4 * g + side
+                rep_out[number, m] = tile.astype(BF16)
+                send(
+                    rep_out.at[number, m], rep_in.at[number, m], m, to_tile(m),
+                    2 + number, 20 + 4 * number + m // PART,
+                )
 
     def extras():
         total = jnp.zeros((M, 2 * CAP), F32)
@@ -272,35 +300,28 @@
                     total = total + dot_t(jnp.where(match, piece, 0.0).astype(BF16), spot)
         ext_out[...] = total.reshape(M, 1, 2 * CAP)
 
-        def post(m, carry):
+        for m in range(M):
             send(ext_out.at[m], ext_in.at[m], m, to_owner(m), 4)
-            return carry
-
-        lax.fori_loop(0, M, post, 0)
 
     def collect_extras():
-        row, lane = iota((32, 256), 0), iota((32, 256), 1)
-        part, group = row >> 3, row & 3
-        right = ((lane & (2 * CAP - 1)) >= CAP).astype(I32)
-        wanted = jnp.logical_or(
-            jnp.logical_and(part < 3, ((row >> 2) & 1) == right),
-            jnp.logical_and(part == 3, jnp.logical_and(right == 0, ((row >> 2) & 1) == (lane >> 7))),
-        )
-        wanted = jnp.where(wanted, group, -2)
-
-        def pair(i, carry):
-            index = jnp.concatenate([req_in[2 * i], req_in[2 * i + 1]], axis=1)
-            value = jnp.concatenate([ext_in[2 * i], ext_in[2 * i + 1]], axis=1)
+        row, lane = iota((40, 256), 0), iota((40, 256), 1)
+        block = row & 3
+        second = ((row >> 2) & 1) == 1
+        wanted = jnp.where(jnp.logical_or(row < 24, ((row - 24) >> 2) == (lane >> 6)), block, -2)
+
+        total = jnp.zeros((32, 256), F32)
+        for g in range(G):
+            norms, shines = unpack4(ext_in, g)
+            value = jnp.where(second, shines, norms)
             high, middle, low = split3(value)
-            picked = jnp.where(part == 0, high, jnp.where(part == 1, middle, jnp.where(part == 2, low, 1.0)))
-            keep = wanted == (index >> 8)
-            lanes = pl.ds(pl.multiple_of(i * 256, 256), 256)
+            picked = jnp.where(row < 8, high, jnp.where(row < 16, middle, jnp.where(row < 24, low, 1.0)))
+            keep = wanted == (owner_row[g] >> 8)
+            lanes = slice(g * 256, g * 256 + 256)
             found = dot_t(jnp.where(keep, picked, 0.0).astype(BF16), owner_hot[:, lanes])
-            counts[slot_at(2 * i)] = found[24:28]
-            counts[slot_at(2 * i + 1)] = found[28:32]
-            return carry + found
-
-        dense_ext[...] = lax.fori_loop(0, MH, pair, jnp.zeros((32, 256), F32))
+            for side in range(4):
+                counts[slot_at(4 * g + side)] = found[24 + 4 * side : 28 + 4 * side]
+            total = total + found[:32]
+        dense_ext[...] = total
         for q in range(4):
             counts_b[q] = counts[:, q, :].astype(BF16)
 
@@ -309,22 +330,26 @@
         answer(number == 0, number)
         if number == 0:
             extras()
-        wait_in(rep_in.at[number], 2 + number)
+
+        def unpack(g, carry):
+            for half, block in enumerate(unpack4(rep_in.at[number], g)):
+                unpacked[half, g] = block.astype(BF16)
+            return carry
+
+        for part in range(4):
+            wait_in(rep_in.at[number, pl.ds(part * PART, PART)], 20 + 4 * number + part)
+            lax.fori_loop(part * G // 4, (part + 1) * G // 4, unpack, 0, unroll=4)
 
         def pick(half):
             def chunk_of(chunk, carry):
                 lanes = pl.ds(pl.multiple_of(chunk * 256, 256), 256)
-                low = rep_in[number, :MH].reshape(MH * 16, 128)
-                top = rep_in[number, MH:].reshape(MH * 16, 128)
-                found = dot(jnp.concatenate([low, top], axis=1), tile_hot[half, :, lanes])
-                who = slot_m[chunk]
-                who = jnp.where(who >= MH, who - MH, who)
-                found = found.reshape(MH, 16, 256)
-                kept = jnp.where(iota((MH, 16, 256), 0) == who.reshape(1, 1, 256), found, 0.0)
+                found = dot(unpacked[half].reshape(G * 16, 256), tile_hot[:, lanes]).reshape(G, 16, 256)
+                group = slot_m[chunk] >> 2
+                kept = jnp.where(iota((G, 16, 256), 0) == group.reshape(1, 1, 256), found, 0.0)
                 cop[number, half, chunk] = jnp.sum(kept, axis=0).astype(BF16)
                 return carry
 
-            lax.fori_loop(0, NCH, chunk_of, 0)
+            lax.fori_loop(0, NCH, chunk_of, 0, unroll=4)
 
         pick(1 - a)
         copy = to_sibling(cop.at[number, 1 - a], cop_in.at[number], 5 + number)
@@ -339,7 +364,7 @@
             raw_terms[chunk] = raw
             return carry[0] + piece_light[chunk] * copies.astype(F32), carry[1] + raw
 
-        lit, level = lax.fori_loop(0, NCH, term, (jnp.zeros((16, 256), F32), jnp.zeros((16, 256), F32)))
+        lit, level = lax.fori_loop(0, NCH, term, (jnp.zeros((16, 256), F32), jnp.zeros((16, 256), F32)), unroll=4)
         level = (jnp.sum(level, axis=1, keepdims=True) * (1.0 / S)).astype(BF16).astype(F32)
         for chunk in range(NCH):
             terms[number, a, chunk] = (raw_terms[chunk] - level).astype(BF16)
@@ -358,33 +383,34 @@
         def scatter(half):
             def fill(chunk, carry):
                 lanes = pl.ds(pl.multiple_of(chunk * 256, 256), 256)
-                who = slot_m[chunk]
-                who = jnp.where(who >= MH, who - MH, who)
+                group = slot_m[chunk] >> 2
                 value = terms[number, half, chunk].astype(F32)
-                mask = iota((MH, 16, 256), 0) == who.reshape(1, 1, 256)
+                mask = iota((G, 16, 256), 0) == group.reshape(1, 1, 256)
                 kept = jnp.where(mask, value.reshape(1, 16, 256), 0.0)
-                spread[:, lanes] = kept.reshape(MH * 16, 256).astype(BF16)
+                spread[:, lanes] = kept.reshape(G * 16, 256).astype(BF16)
                 return carry
 
-            lax.fori_loop(0, NCH, fill, 0)
-            return dot_t(spread[...], tile_hot[half])
-
-        first = scatter(a)
+            lax.fori_loop(0, NCH, fill, 0, unroll=2)
+            packed[half] = dot_t(spread[...], tile_hot[...]).reshape(G, 16, 256)
+
+        scatter(a)
         copy.wait_recv()
-        total = (first + scatter(1 - a)).astype(BF16)
-        send_out[number, :MH] = total[:, :128].reshape(MH, 16, 128)
-        send_out[number, MH:] = total[:, 128:].reshape(MH, 16, 128)
+        scatter(1 - a)
         row_copy.wait_recv()
         num_row_in[number] = num_row[number, 0] + num_row[number, 1]
         tile_parity = (x + y + z) % 2
         tile_slot = tile_parity * M + (x * Y + y) * ZH + z // 2
 
-        def post(m, carry):
-            send(send_out.at[number, m], send_in.at[number, m], m, to_owner(m), 11 + number)
+        for g in range(G):
+            for side, tile in enumerate(pack4(packed[0, g], packed[1, g])):
+                m = 4 * g + side
+                send_out[number, m] = tile.astype(BF16)
+                send(
+                    send_out.at[number, m], send_in.at[number, m], m, to_owner(m),
+                    11 + number, 28 + 4 * number + m // PART,
+                )
+        for m in range(M):
             send(num_row_in.at[number], num_in.at[number, tile_slot], m, to_owner(m), 13 + number)
-            return carry
-
-        lax.fori_loop(0, M, post, 0)
 
         if number == 0:
             wait_in(ext_in, 4)
@@ -393,29 +419,29 @@
             pending.append(ext_copy)
             mixing_load.wait()
 
+        sums = jnp.zeros((128, 256), F32)
+        for part in range(4):
+            wait_in(send_in.at[number, pl.ds(part * PART, PART)], 28 + 4 * number + part)
+
+            def gather_rows(g, carry):
+                block = owner_row[g] >> 8
+                lanes = pl.ds(pl.multiple_of(g * 256, 256), 256)
+                for half, value in enumerate(unpack4(send_in.at[number], g)):
+                    for q in range(4):
+                        at = (half * 4 + q) * 16
+                        gathered[at : at + 16, lanes] = jnp.where(block == q, value, 0.0).astype(BF16)
+                return carry
+
+            lax.fori_loop(part * G // 4, (part + 1) * G // 4, gather_rows, 0, unroll=4)
+            lanes = slice(part * PART * CAP, (part + 1) * PART * CAP)
+            sums = sums + dot_t(gathered[:, lanes], owner_hot[:, lanes])
+        sums = sums.reshape(2, 4, 16, 256)
+
         half_at = ((x + y + z + a) % 2) * M
         mine = num_in.at[number, pl.ds(half_at, M)]
         wait_in(mine, 13 + number)
         num_copy = to_sibling(mine, mine, 16 + number)
         pending.append(num_copy)
-
-        wait_in(send_in.at[number], 11 + number)
-        right = (iota((1, 256), 1) & (2 * CAP - 1)) >= CAP
-
-        def gather_rows(i, carry):
-            index = jnp.concatenate([req_in[2 * i], req_in[2 * i + 1]], axis=1)
-            value = jnp.concatenate([send_in[number, 2 * i], send_in[number, 2 * i + 1]], axis=1).astype(F32)
-            group = index >> 8
-            lanes = pl.ds(pl.multiple_of(i * 256, 256), 256)
-            for half in range(2):
-                for q in range(4):
-                    keep = jnp.logical_and(group == q, right if half else jnp.logical_not(right))
-                    at = (half * 4 + q) * 16
-                    gathered[at : at + 16, lanes] = jnp.where(keep, value, 0.0).astype(BF16)
-            return carry
-
-        lax.fori_loop(0, MH, gather_rows, 0)
-        sums = dot_t(gathered[...], owner_hot[...]).reshape(2, 4, 16, 256)
         levels = jnp.transpose(mine[...].reshape(M, 128))[64:96].astype(BF16)
         for q in range(4):
             dense[number, :, q] = sums[:, q] + dot(levels, counts_b[q]).reshape(2, 16, 256)
@@ -495,21 +521,21 @@
         scratch = [
             V((cells * frames, pixels), BF16), V((S, pixels), BF16), V((cells, pixels), BF16),
             V((1024, own), BF16), pltpu.SemaphoreType.DMA((10,)),
-            V((NCH, 1, 256), I32), V((NCH, 1, 256), I32), V((2, 256, S), BF16),
-            V((M, 1, 128), I32), V((M, 1, 128), I32), V((256, M * 128), BF16),
+            V((NCH, 1, 256), I32), V((NCH, 1, 256), I32), V((256, S), BF16),
+            V((M, 1, 128), I32), V((M, 1, 128), I32), V((256, M * CAP), BF16), V((M // 4, 1, 256), I32),
             V((2, 16, own), F32), V((4, 2, 16, 256), F32), V((2, 4, 16, 256), BF16),
             V((2, NCH, 256, 256), BF16), V((NCH, 16, 256), F32), V((NCH, 1, 256), F32),
             V((NCH, 1, 256), F32), V((16, 1), F32),
             V((M, 1, 128), F32), V((M, 1, 128), F32), V((32, 256), F32), V((32, 256), F32),
             V((M, 4, 256), F32), V((4, M, 256), BF16), V((NCH, 16, 256), F32),
-            V((PASSES, M, 16, 128), BF16), V((PASSES, M, 16, 128), BF16),
+            V((PASSES, M, 16, 128), BF16), V((PASSES, M, 16, 128), BF16), V((2, M // 4, 16, 256), BF16),
             V((PASSES, 2, NCH, 16, 256), BF16), V((PASSES, NCH, 16, 256), BF16),
             V((PASSES, 2, NCH, 16, 256), BF16),
             V((PASSES, 2, 1, 128), F32), V((PASSES, 1, 128), F32),
-            V((M * 8, S), BF16), V((PASSES, M, 16, 128), BF16), V((PASSES, M, 16, 128), BF16),
-            V((PASSES, 2 * M, 1, 128), F32), V((128, M * 128), BF16),
+            V((M * 4, S), BF16), V((2, M // 4, 16, 256), F32), V((PASSES, M, 16, 128), BF16), V((PASSES, M, 16, 128), BF16),
+            V((PASSES, 2 * M, 1, 128), F32), V((128, M * CAP), BF16),
             V((PASSES, 2, 4, 16, 256), F32), V((PASSES, 2, 4, 16, 256), F32),
-            pltpu.SemaphoreType.DMA((20,)), pltpu.SemaphoreType.DMA((20,)),
+            pltpu.SemaphoreType.DMA((20,)), pltpu.SemaphoreType.DMA((36,)),
         ]
         result, background = pl.pallas_call(
             functools.partial(kernel, (X, Y, Z, S)),

time: 104 us -> 84.3 us (0.81)
  Pallas kernels: 100 us -> 80.9 us
    pallas_call x1, Pallas kernels: 100 us -> 80.9 us  [body(): pl.pallas_call(functools.partial(kernel, (X, Y, Z, S)), out_shape=(jax.Sh...]
where the time goes in v2:
time: 84.3 us; the launch traced here: 84.1 us
  Pallas kernels  80.9 us (96%)
  local copies, waits for them, and re-layouts  2.59 us (3%)
    pallas_call x1, Pallas kernels, body(): pl.pallas_call(functools.partial(kernel, (X, Y, Z, S)), out_shape=(jax.Sh...  80.9 us

profile of v2, /device:TPU:1, one launch (start us, length us, event | category | flops | bytes accessed | tf_op | source)
XLA Modules:
  0.0 84.1 jit_solution(11170855311977910691)
XLA Ops:
  0.6 80.9 %cnmf_passes.1 = (f32[16,1024]{1,0:T(8,128)}, f32[1,128]{1,0:T(1,128)}) custom-call(bf16[2048,1024]{1,0:T(8,128)(2,1)} %bitcast.10, bf16[2048,1024]{1,0:T(8,128)(2,1)} %bitcast.11, bf16[128,1024]{1,0:T(8,128)(2,1)} %bitcast.13, bf16[1024,1024]{1,0:T(8,128)(2,1)} %bitcast.12, s32[1,2048]{1,0:T(1,128)} %bitcast.14, s32[1,2048]{1,0:T(1,128)} %bitcast.15, ...), custom_call_target="tpu_custom_call" | custom-call | tf_op jit(solution)/shard_map/cnmf_passes/pallas_call | solution.py:540
  81.6 1.1 %slice_bitcast_fusion = f32[16]{0:T(128)} fusion(f32[1,128]{1,0:T(1,128)} %get-tuple-element.5), kind=kLoop, calls=%fused_computation | loop fusion | bytes 128 | tf_op jit(solution)/shard_map/squeeze | solution.py:564
  82.7 1.5 %copy.12 = f32[16,1024]{1,0:T(8,128)} copy(f32[16,1024]{1,0:T(8,128)} %get-tuple-element.8) | data formatting | bytes 131072

commit v3 on v2

--- a/solution.py
+++ b/solution.py
@@ -11,6 +11,7 @@
 DECONV_ITERS = 3
 PASSES = 2
 CAP = 64
+EARLY = 2
 MESH = pl.DeviceIdType.MESH
 F32, BF16, I32 = jnp.float32, jnp.bfloat16, jnp.int32
 
@@ -35,9 +36,9 @@
 
 def kernel(
     dims,
-    movie_h, pieces_h, light_h, mixing_h, owner_ref, offset_ref, traces_ref, ar1_ref, ar2_ref,
+    movie_h, pieces_h, light_h, mixing_h, owner_h, offset_h, traces_h, ar1_h, ar2_h,
     out_ref, bg_ref,
-    movie, pieces, light, mixing, load_sems,
+    movie, pieces, light, mixing, owner_ref, offset_ref, ar1_ref, ar2_ref, mixing_wide, mixing_turned, driven, load_sems,
     slot_m, slot_j, tile_hot, req_out, req_in, owner_hot, owner_row,
     both_traces, current, current_b,
     block_gram, piece_movie, piece_light, piece_norm, light_movie,
@@ -130,13 +131,36 @@
         def _():
             pltpu.make_async_copy(buffer, buffer, send_sems.at[sem]).wait()
 
-    def to_sibling(source, target, sem):
+    def to_sibling(source, target, sem, recv=None):
+        recv = sem if recv is None else recv
         copy = pltpu.make_async_remote_copy(
-            source, target, send_sems.at[sem], recv_sems.at[sem], device_id=sibling, device_id_type=MESH
+            source, target, send_sems.at[sem], recv_sems.at[recv], device_id=sibling, device_id_type=MESH
         )
         copy.start()
         return copy
 
+    barrier = pltpu.get_barrier_semaphore()
+
+    pl.semaphore_signal(barrier, inc=1, device_id=sibling, device_id_type=MESH)
+    for m in range(M):
+        if m != self_m:
+            pl.semaphore_signal(barrier, inc=1, device_id=to_owner(m), device_id_type=MESH)
+
+    @pl.when(a == 1)
+    def _():
+        pl.semaphore_signal(barrier, inc=1, device_id=to_owner(self_m), device_id_type=MESH)
+
+    index_loads = [
+        pltpu.make_async_copy(owner_h, owner_ref, load_sems.at[10]),
+        pltpu.make_async_copy(offset_h, offset_ref, load_sems.at[11]),
+    ]
+    traces_load = pltpu.make_async_copy(traces_h, both_traces.at[a], load_sems.at[12])
+    lag_loads = [
+        pltpu.make_async_copy(ar1_h, ar1_ref, load_sems.at[13]),
+        pltpu.make_async_copy(ar2_h, ar2_ref, load_sems.at[14]),
+    ]
+    for copy in index_loads + [traces_load]:
+        copy.start()
     loads = []
     rows = movie.shape[0] // 4
     light_load = pltpu.make_async_copy(light_h, light, load_sems.at[8])
@@ -152,17 +176,10 @@
         loads.append(pair)
     mixing_load = pltpu.make_async_copy(mixing_h, mixing, load_sems.at[9])
     mixing_load.start()
-
-    barrier = pltpu.get_barrier_semaphore()
-
-    pl.semaphore_signal(barrier, inc=1, device_id=sibling, device_id_type=MESH)
-    for m in range(M):
-        if m != self_m:
-            pl.semaphore_signal(barrier, inc=1, device_id=to_owner(m), device_id_type=MESH)
-
-    @pl.when(a == 1)
-    def _():
-        pl.semaphore_signal(barrier, inc=1, device_id=to_owner(self_m), device_id_type=MESH)
+    for copy in lag_loads:
+        copy.start()
+    for copy in index_loads:
+        copy.wait()
 
     own_of = owner_ref[...]
     far = own_of // Z
@@ -203,22 +220,6 @@
         asked = asked + dot_t(halves, where_to)
     req_out[...] = ((asked[:M] * 32.0 + asked[M:]).astype(I32) - 1).reshape(M, 1, 2 * CAP)
 
-    pl.semaphore_wait(barrier, M + a)
-    both_traces[a] = traces_ref[...]
-    trace_copy = to_sibling(both_traces.at[a], both_traces.at[a], 0)
-
-    for m in range(M):
-        send(req_out.at[m], req_in.at[m], m, to_owner(m), 1)
-
-    def tile_maps(chunk, carry):
-        who, rank = slot_m[chunk], slot_j[chunk]
-        lanes = pl.ds(pl.multiple_of(chunk * 256, 256), 256)
-        row = jnp.where(who >= 0, (who & 3) * CAP + rank, -1)
-        tile_hot[:, lanes] = jnp.where(iota((256, 256), 0) == row, 1.0, 0.0).astype(BF16)
-        return carry
-
-    lax.fori_loop(0, NCH, tile_maps, 0, unroll=2)
-
     light_load.wait()
     same_cell = (iota((256, 256), 0) >> 4) == (iota((256, 256), 1) >> 4)
     diagonal = iota((256, 256), 0) == iota((256, 256), 1)
@@ -244,10 +245,33 @@
         return numer, energy + lit_f * lit_f
 
     carry = (jnp.zeros((16, 16), F32), jnp.zeros((16, 1024), F32))
-    for part in range(4):
+
+    def gram_part(part, carry):
         for copy in loads[part]:
             copy.wait()
-        carry = lax.fori_loop(part * NCH // 4, (part + 1) * NCH // 4, gram, carry, unroll=2)
+        return lax.fori_loop(part * NCH // 4, (part + 1) * NCH // 4, gram, carry, unroll=2)
+
+    for part in range(EARLY):
+        carry = gram_part(part, carry)
+
+    pl.semaphore_wait(barrier, M + a)
+    traces_load.wait()
+    trace_copy = to_sibling(both_traces.at[a], both_traces.at[a], 0)
+
+    for m in range(M):
+        send(req_out.at[m], req_in.at[m], m, to_owner(m), 1, 36 + m // PART)
+
+    def tile_maps(chunk, carry):
+        who, rank = slot_m[chunk], slot_j[chunk]
+        lanes = pl.ds(pl.multiple_of(chunk * 256, 256), 256)
+        row = jnp.where(who >= 0, (who & 3) * CAP + rank, -1)
+        tile_hot[:, lanes] = jnp.where(iota((256, 256), 0) == row, 1.0, 0.0).astype(BF16)
+        return carry
+
+    lax.fori_loop(0, NCH, tile_maps, 0, unroll=2)
+
+    for part in range(EARLY, 4):
+        carry = gram_part(part, carry)
     light_movie[...] = jnp.sum(carry[0], axis=1, keepdims=True)
     energy = jnp.sum(jnp.sum(carry[1], axis=1, keepdims=True), axis=0, keepdims=True)
 
@@ -258,12 +282,14 @@
             part = both_traces[half, :, lanes]
             current[q, half] = part
             current_b[half, q] = part.astype(BF16)
-    wait_in(req_in, 1)
 
     def answer(build, number):
-        for g in range(G):
+        for g in reversed(range(G)) if build else range(G):
             lanes = slice(g * 256, g * 256 + 256)
             if build:
+                if (4 * g + 4) % PART == 0:
+                    part = (4 * g + 4) // PART - 1
+                    wait_in(req_in.at[pl.ds(part * PART, PART)], 36 + part)
                 asked_for = [req_in[4 * g + side] for side in range(4)]
                 index = jnp.concatenate(
                     [jnp.where(left, asked_for[0], asked_for[1]), jnp.where(left, asked_for[2], asked_for[3])], axis=1
@@ -325,6 +351,29 @@
         for q in range(4):
             counts_b[q] = counts[:, q, :].astype(BF16)
 
+    def turn_mixing():
+        mixing_load.wait()
+
+        def widen(i, carry):
+            rows = pl.ds(pl.multiple_of(i * 32, 32), 32)
+            wide = mixing[rows, :].astype(F32)
+            for part in range(8):
+                at = pl.ds(pl.multiple_of(part * 1024 + i * 32, 32), 32)
+                mixing_wide[at, :] = wide[:, part * 128 : part * 128 + 128]
+            return carry
+
+        lax.fori_loop(0, 32, widen, 0, unroll=2)
+
+        def turn(i, carry):
+            for part in range(8):
+                lanes = slice(part * 128, part * 128 + 128)
+                mixing_turned[pl.ds(pl.multiple_of(i * 32, 32), 32), lanes] = mixing_wide[
+                    pl.ds(part * 1024 + i, 32, stride=32), :
+                ]
+            return carry
+
+        lax.fori_loop(0, 32, turn, 0, unroll=2)
+
     pending = []
     for number in range(PASSES):
         answer(number == 0, number)
@@ -340,7 +389,7 @@
             wait_in(rep_in.at[number, pl.ds(part * PART, PART)], 20 + 4 * number + part)
             lax.fori_loop(part * G // 4, (part + 1) * G // 4, unpack, 0, unroll=4)
 
-        def pick(half):
+        def pick(half, first, last):
             def chunk_of(chunk, carry):
                 lanes = pl.ds(pl.multiple_of(chunk * 256, 256), 256)
                 found = dot(unpacked[half].reshape(G * 16, 256), tile_hot[:, lanes]).reshape(G, 16, 256)
@@ -349,13 +398,16 @@
                 cop[number, half, chunk] = jnp.sum(kept, axis=0).astype(BF16)
                 return carry
 
-            lax.fori_loop(0, NCH, chunk_of, 0, unroll=4)
-
-        pick(1 - a)
-        copy = to_sibling(cop.at[number, 1 - a], cop_in.at[number], 5 + number)
-        pick(a)
-        copy.wait_recv()
-        pending.append(copy)
+            lax.fori_loop(first, last, chunk_of, 0, unroll=4)
+
+        moved = []
+        for part in range(2):
+            first, last = part * NCH // 2, (part + 1) * NCH // 2
+            pick(1 - a, first, last)
+            span = pl.ds(first, last - first)
+            moved.append(to_sibling(cop.at[number, 1 - a, span], cop_in.at[number, span], (5, 16)[part] + number))
+        pick(a, 0, NCH)
+        pending.extend(moved)
 
         def term(chunk, carry):
             copies = cop[number, a, chunk] + cop_in[number, chunk]
@@ -364,7 +416,11 @@
             raw_terms[chunk] = raw
             return carry[0] + piece_light[chunk] * copies.astype(F32), carry[1] + raw
 
-        lit, level = lax.fori_loop(0, NCH, term, (jnp.zeros((16, 256), F32), jnp.zeros((16, 256), F32)), unroll=4)
+        lit_level = (jnp.zeros((16, 256), F32), jnp.zeros((16, 256), F32))
+        for part in range(2):
+            moved[part].wait_recv()
+            lit_level = lax.fori_loop(part * NCH // 2, (part + 1) * NCH // 2, term, lit_level, unroll=4)
+        lit, level = lit_level
         level = (jnp.sum(level, axis=1, keepdims=True) * (1.0 / S)).astype(BF16).astype(F32)
         for chunk in range(NCH):
             terms[number, a, chunk] = (raw_terms[chunk] - level).astype(BF16)
@@ -409,18 +465,25 @@
                     send_out.at[number, m], send_in.at[number, m], m, to_owner(m),
                     11 + number, 28 + 4 * number + m // PART,
                 )
-        for m in range(M):
-            send(num_row_in.at[number], num_in.at[number, tile_slot], m, to_owner(m), 13 + number)
+                send(num_row_in.at[number], num_in.at[number, tile_slot], m, to_owner(m), 13 + number)
 
         if number == 0:
             wait_in(ext_in, 4)
+            turn_mixing()
             collect_extras()
             ext_copy = to_sibling(dense_ext, dense_ext_in, 15)
             pending.append(ext_copy)
-            mixing_load.wait()
+            for copy in lag_loads:
+                copy.wait()
 
         sums = jnp.zeros((128, 256), F32)
         for part in range(4):
+            if part == 3:
+                half_at = ((x + y + z + a) % 2) * M
+                mine = num_in.at[number, pl.ds(half_at, M)]
+                wait_in(mine, 13 + number)
+                num_copy = to_sibling(mine, mine, 20 + number, 40 + number)
+                pending.append(num_copy)
             wait_in(send_in.at[number, pl.ds(part * PART, PART)], 28 + 4 * number + part)
 
             def gather_rows(g, carry):
@@ -437,11 +500,6 @@
             sums = sums + dot_t(gathered[:, lanes], owner_hot[:, lanes])
         sums = sums.reshape(2, 4, 16, 256)
 
-        half_at = ((x + y + z + a) % 2) * M
-        mine = num_in.at[number, pl.ds(half_at, M)]
-        wait_in(mine, 13 + number)
-        num_copy = to_sibling(mine, mine, 16 + number)
-        pending.append(num_copy)
         levels = jnp.transpose(mine[...].reshape(M, 128))[64:96].astype(BF16)
         for q in range(4):
             dense[number, :, q] = sums[:, q] + dot(levels, counts_b[q]).reshape(2, 16, 256)
@@ -479,18 +537,19 @@
                 dual = dual + filtered - spikes
                 drive = spikes - dual
                 drive = target + (drive - g1 * ahead(drive, 1) - g2 * ahead(drive, 2))
-                parts = []
-                for block in range(4):
-                    matrix = mixing[block * 256 : block * 256 + 256, lanes].astype(F32).reshape(8, 32, 256)
-                    parts.append(jnp.sum(matrix * drive.reshape(1, 32, 256), axis=1))
-                latest = jnp.concatenate(parts, axis=0)
-            latest = latest.reshape(2, 16, 256)
-            current[q] = latest
+                driven[...] = drive
+                last = number == PASSES - 1 and sweep == DECONV_ITERS - 1
+                latest = jnp.zeros((16 if last else 32, 256), F32)
+                for s in range(32):
+                    rows = pl.ds(pl.multiple_of(s * 32 + 16 * a, 16), 16) if last else pl.ds(s * 32, 32)
+                    latest = latest + mixing_turned[rows, lanes] * driven[s : s + 1, :]
             if number < PASSES - 1:
+                latest = latest.reshape(2, 16, 256)
+                current[q] = latest
                 current_b[:, q] = latest.astype(BF16)
+            else:
+                out_ref[:, lanes] = latest
         if number == PASSES - 1:
-            for q in range(4):
-                out_ref[:, q * 256 : q * 256 + 256] = current[q, a]
             own = iota((32, 128), 0) == iota((32, 128), 1) + 16 * a
             bg_ref[...] = jnp.sum(jnp.where(own, bg, 0.0), axis=0, keepdims=True)
 
@@ -520,7 +579,9 @@
         V = pltpu.VMEM
         scratch = [
             V((cells * frames, pixels), BF16), V((S, pixels), BF16), V((cells, pixels), BF16),
-            V((1024, own), BF16), pltpu.SemaphoreType.DMA((10,)),
+            V((1024, own), BF16), V((1, S), I32), V((1, S), I32), V((1, own), F32), V((1, own), F32),
+            V((own * 8, 128), F32), V((1024, own), F32), V((32, 256), F32),
+            pltpu.SemaphoreType.DMA((15,)),
             V((NCH, 1, 256), I32), V((NCH, 1, 256), I32), V((256, S), BF16),
             V((M, 1, 128), I32), V((M, 1, 128), I32), V((256, M * CAP), BF16), V((M // 4, 1, 256), I32),
             V((2, 16, own), F32), V((4, 2, 16, 256), F32), V((2, 4, 16, 256), BF16),
@@ -535,7 +596,7 @@
             V((M * 4, S), BF16), V((2, M // 4, 16, 256), F32), V((PASSES, M, 16, 128), BF16), V((PASSES, M, 16, 128), BF16),
             V((PASSES, 2 * M, 1, 128), F32), V((128, M * CAP), BF16),
             V((PASSES, 2, 4, 16, 256), F32), V((PASSES, 2, 4, 16, 256), F32),
-            pltpu.SemaphoreType.DMA((20,)), pltpu.SemaphoreType.DMA((36,)),
+            pltpu.SemaphoreType.DMA((22,)), pltpu.SemaphoreType.DMA((44,)),
         ]
         result, background = pl.pallas_call(
             functools.partial(kernel, (X, Y, Z, S)),
@@ -543,7 +604,7 @@
                 jax.ShapeDtypeStruct((frames, own), F32),
                 jax.ShapeDtypeStruct((1, 128), F32),
             ),
-            in_specs=[any_spec] * 4 + [vmem_spec] * 5,
+            in_specs=[any_spec] * 9,
             out_specs=(vmem_spec, vmem_spec),
             scratch_shapes=scratch,
             compiler_params=pltpu.CompilerParams(

time: 84.3 us -> 80.1 us (0.950)
  Pallas kernels: 80.9 us -> 76.7 us
    pallas_call x1, Pallas kernels: 80.9 us -> 76.7 us  [body(): pl.pallas_call(functools.partial(kernel, (X, Y, Z, S)), out_shape=(jax.Sh...]
where the time goes in v3:
time: 80.1 us; the launch traced here: 79.9 us
  Pallas kernels  76.7 us (96%)
  local copies, waits for them, and re-layouts  2.59 us (3%)
    pallas_call x1, Pallas kernels, body(): pl.pallas_call(functools.partial(kernel, (X, Y, Z, S)), out_shape=(jax.Sh...  76.7 us

profile of v3, /device:TPU:1, one launch (start us, length us, event | category | flops | bytes accessed | tf_op | source)
XLA Modules:
  0.0 79.9 jit_solution(15303001909695532870)
XLA Ops:
  0.6 76.7 %cnmf_passes.1 = (f32[16,1024]{1,0:T(8,128)}, f32[1,128]{1,0:T(1,128)}) custom-call(bf16[2048,1024]{1,0:T(8,128)(2,1)} %bitcast.10, bf16[2048,1024]{1,0:T(8,128)(2,1)} %bitcast.11, bf16[128,1024]{1,0:T(8,128)(2,1)} %bitcast.13, bf16[1024,1024]{1,0:T(8,128)(2,1)} %bitcast.12, s32[1,2048]{1,0:T(1,128)} %bitcast.14, s32[1,2048]{1,0:T(1,128)} %bitcast.15, ...), custom_call_target="tpu_custom_call" | custom-call | tf_op jit(solution)/shard_map/cnmf_passes/pallas_call | solution.py:601
  77.3 1.1 %slice_bitcast_fusion = f32[16]{0:T(128)} fusion(f32[1,128]{1,0:T(1,128)} %get-tuple-element.5), kind=kLoop, calls=%fused_computation | loop fusion | bytes 128 | tf_op jit(solution)/shard_map/squeeze | solution.py:625
  78.4 1.5 %copy.12 = f32[16,1024]{1,0:T(8,128)} copy(f32[16,1024]{1,0:T(8,128)} %get-tuple-element.8) | data formatting | bytes 131072

commit v4 on v3

--- a/solution.py
+++ b/solution.py
@@ -67,21 +67,25 @@
     number_of = [order.index(i) for i in range(M)]
     self_m = number_of[0]
 
-    def displacement(m):
+    odd = [a, 1 - a]
+    owner_x = [lax.rem(x + d, X) * Y for d in range(X)]
+    owner_y = [lax.rem(y + d, Y) for d in range(Y)]
+    owner_z = [[lax.rem(z + 2 * d + bit, Z) for bit in odd] for d in range(ZH)]
+    tile_x = [lax.rem(x + X - d, X) * Y for d in range(X)]
+    tile_y = [lax.rem(y + Y - d, Y) for d in range(Y)]
+    tile_z = [[lax.rem(z + Z - 2 * d - bit, Z) for bit in odd] for d in range(ZH)]
+
+    def to_owner(m):
         dx, dy, half_dz = places[order[m]]
-        return dx, dy, 2 * half_dz + (dx + dy + a) % 2
-
-    def to_owner(m):
-        dx, dy, dz = displacement(m)
-        return ((x + dx) % X) * Y + (y + dy) % Y, (z + dz) % Z, a
+        return owner_x[dx] + owner_y[dy], owner_z[half_dz][(dx + dy) % 2], a
 
     def to_tile(m):
-        dx, dy, dz = displacement(m)
-        return ((x + X - dx) % X) * Y + (y + Y - dy) % Y, (z + Z - dz) % Z, a
+        dx, dy, half_dz = places[order[m]]
+        return tile_x[dx] + tile_y[dy], tile_z[half_dz][(dx + dy) % 2], a
 
     def slot_at(m):
-        dx, dy, dz = displacement(m)
-        return (((x + X - dx) % X) * Y + (y + Y - dy) % Y) * ZH + ((z + Z - dz) % Z) // 2
+        dx, dy, half_dz = places[order[m]]
+        return (tile_x[dx] + tile_y[dy]) * ZH + lax.div(tile_z[half_dz][(dx + dy) % 2], 2)
 
     def send(source, target, m, peer, sem, recv=None):
         recv = sem if recv is None else recv
@@ -268,7 +272,7 @@
         tile_hot[:, lanes] = jnp.where(iota((256, 256), 0) == row, 1.0, 0.0).astype(BF16)
         return carry
 
-    lax.fori_loop(0, NCH, tile_maps, 0, unroll=2)
+    lax.fori_loop(0, NCH, tile_maps, 0, unroll=4)
 
     for part in range(EARLY, 4):
         carry = gram_part(part, carry)
@@ -284,11 +288,11 @@
             current_b[half, q] = part.astype(BF16)
 
     def answer(build, number):
-        for g in reversed(range(G)) if build else range(G):
+        for g in range(G):
             lanes = slice(g * 256, g * 256 + 256)
             if build:
-                if (4 * g + 4) % PART == 0:
-                    part = (4 * g + 4) // PART - 1
+                if (4 * g) % PART == 0:
+                    part = 4 * g // PART
                     wait_in(req_in.at[pl.ds(part * PART, PART)], 36 + part)
                 asked_for = [req_in[4 * g + side] for side in range(4)]
                 index = jnp.concatenate(
@@ -376,9 +380,9 @@
 
     pending = []
     for number in range(PASSES):
-        answer(number == 0, number)
         if number == 0:
             extras()
+        answer(number == 0, number)
 
         def unpack(g, carry):
             for half, block in enumerate(unpack4(rep_in.at[number], g)):
@@ -446,7 +450,7 @@
                 spread[:, lanes] = kept.reshape(G * 16, 256).astype(BF16)
                 return carry
 
-            lax.fori_loop(0, NCH, fill, 0, unroll=2)
+            lax.fori_loop(0, NCH, fill, 0, unroll=8)
             packed[half] = dot_t(spread[...], tile_hot[...]).reshape(G, 16, 256)
 
         scatter(a)
@@ -521,34 +525,41 @@
         def ahead(values, lag):
             return jnp.where(frame < 32 - lag, pltpu.roll(values, 32 - lag, 0), 0.0)
 
-        for q in range(4):
-            lanes = slice(q * 256, q * 256 + 256)
-            ext = dense_ext[...] + dense_ext_in[...]
-            weight = ext[q : q + 1] + ext[8 + q : 9 + q] + ext[16 + q : 17 + q]
-            shine = ext[4 + q : 5 + q] + ext[12 + q : 13 + q] + ext[20 + q : 21 + q]
-            summed = (dense[number, :, q] + dense_in[number, :, q]).reshape(32, 256) - bg * shine
-            target = current[q].reshape(32, 256) + summed / jnp.maximum(weight, 1.0)
-            g1, g2 = ar1_ref[:, lanes], ar2_ref[:, lanes]
-            latest = target
-            dual = jnp.zeros_like(target)
+        for pair in range(2):
+            states = []
+            for q in (2 * pair, 2 * pair + 1):
+                lanes = slice(q * 256, q * 256 + 256)
+                ext = dense_ext[...] + dense_ext_in[...]
+                weight = ext[q : q + 1] + ext[8 + q : 9 + q] + ext[16 + q : 17 + q]
+                shine = ext[4 + q : 5 + q] + ext[12 + q : 13 + q] + ext[20 + q : 21 + q]
+                summed = (dense[number, :, q] + dense_in[number, :, q]).reshape(32, 256) - bg * shine
+                target = current[q].reshape(32, 256) + summed / jnp.maximum(weight, 1.0)
+                states.append([q, lanes, target, target, jnp.zeros_like(target)])
             for sweep in range(DECONV_ITERS):
-                filtered = latest - g1 * back(latest, 1) - g2 * back(latest, 2)
-                spikes = jnp.maximum(filtered + dual, 0.0)
-                dual = dual + filtered - spikes
-                drive = spikes - dual
-                drive = target + (drive - g1 * ahead(drive, 1) - g2 * ahead(drive, 2))
-                driven[...] = drive
                 last = number == PASSES - 1 and sweep == DECONV_ITERS - 1
-                latest = jnp.zeros((16 if last else 32, 256), F32)
-                for s in range(32):
-                    rows = pl.ds(pl.multiple_of(s * 32 + 16 * a, 16), 16) if last else pl.ds(s * 32, 32)
-                    latest = latest + mixing_turned[rows, lanes] * driven[s : s + 1, :]
-            if number < PASSES - 1:
-                latest = latest.reshape(2, 16, 256)
-                current[q] = latest
-                current_b[:, q] = latest.astype(BF16)
-            else:
-                out_ref[:, lanes] = latest
+                for state in states:
+                    q, lanes, target, latest, dual = state
+                    g1, g2 = ar1_ref[:, lanes], ar2_ref[:, lanes]
+                    filtered = latest - g1 * back(latest, 1) - g2 * back(latest, 2)
+                    spikes = jnp.maximum(filtered + dual, 0.0)
+                    dual = dual + filtered - spikes
+                    drive = spikes - dual
+                    driven[q * DECONV_ITERS + sweep] = target + (drive - g1 * ahead(drive, 1) - g2 * ahead(drive, 2))
+                    state[4] = dual
+                for state in states:
+                    q, lanes = state[:2]
+                    latest = jnp.zeros((16 if last else 32, 256), F32)
+                    for s in range(32):
+                        rows = pl.ds(pl.multiple_of(s * 32 + 16 * a, 16), 16) if last else pl.ds(s * 32, 32)
+                        latest = latest + mixing_turned[rows, lanes] * driven[q * DECONV_ITERS + sweep, s : s + 1, :]
+                    state[3] = latest
+            for q, lanes, target, latest, dual in states:
+                if number < PASSES - 1:
+                    latest = latest.reshape(2, 16, 256)
+                    current[q] = latest
+                    current_b[:, q] = latest.astype(BF16)
+                else:
+                    out_ref[:, lanes] = latest
         if number == PASSES - 1:
             own = iota((32, 128), 0) == iota((32, 128), 1) + 16 * a
             bg_ref[...] = jnp.sum(jnp.where(own, bg, 0.0), axis=0, keepdims=True)
@@ -580,7 +591,7 @@
         scratch = [
             V((cells * frames, pixels), BF16), V((S, pixels), BF16), V((cells, pixels), BF16),
             V((1024, own), BF16), V((1, S), I32), V((1, S), I32), V((1, own), F32), V((1, own), F32),
-            V((own * 8, 128), F32), V((1024, own), F32), V((32, 256), F32),
+            V((own * 8, 128), F32), V((1024, own), F32), V((4 * DECONV_ITERS, 32, 256), F32),
             pltpu.SemaphoreType.DMA((15,)),
             V((NCH, 1, 256), I32), V((NCH, 1, 256), I32), V((256, S), BF16),
             V((M, 1, 128), I32), V((M, 1, 128), I32), V((256, M * CAP), BF16), V((M // 4, 1, 256), I32),

time: 80.1 us -> 78.6 us (0.981)
  Pallas kernels: 76.7 us -> 75.2 us
    pallas_call x1, Pallas kernels: 76.7 us -> 75.2 us  [body(): pl.pallas_call(functools.partial(kernel, (X, Y, Z, S)), out_shape=(jax.Sh...]
where the time goes in v4:
time: 78.6 us; the launch traced here: 78.4 us
  Pallas kernels  75.2 us (96%)
  local copies, waits for them, and re-layouts  2.59 us (3%)
    pallas_call x1, Pallas kernels, body(): pl.pallas_call(functools.partial(kernel, (X, Y, Z, S)), out_shape=(jax.Sh...  75.2 us

profile of v4, /device:TPU:1, one launch (start us, length us, event | category | flops | bytes accessed | tf_op | source)
XLA Modules:
  0.0 78.4 jit_solution(5083402907451634650)
XLA Ops:
  0.6 75.2 %cnmf_passes.1 = (f32[16,1024]{1,0:T(8,128)}, f32[1,128]{1,0:T(1,128)}) custom-call(bf16[2048,1024]{1,0:T(8,128)(2,1)} %bitcast.10, bf16[2048,1024]{1,0:T(8,128)(2,1)} %bitcast.11, bf16[128,1024]{1,0:T(8,128)(2,1)} %bitcast.13, bf16[1024,1024]{1,0:T(8,128)(2,1)} %bitcast.12, s32[1,2048]{1,0:T(1,128)} %bitcast.14, s32[1,2048]{1,0:T(1,128)} %bitcast.15, ...), custom_call_target="tpu_custom_call" | custom-call | tf_op jit(solution)/shard_map/cnmf_passes/pallas_call | solution.py:612
  75.8 1.1 %slice_bitcast_fusion = f32[16]{0:T(128)} fusion(f32[1,128]{1,0:T(1,128)} %get-tuple-element.5), kind=kLoop, calls=%fused_computation | loop fusion | bytes 128 | tf_op jit(solution)/shard_map/squeeze | solution.py:636
  77.0 1.5 %copy.12 = f32[16,1024]{1,0:T(8,128)} copy(f32[16,1024]{1,0:T(8,128)} %get-tuple-element.8) | data formatting | bytes 131072
